TPU v7x, 768 devices: a whole 4x8x12 slice. The times are simulated.
768 devices in a mesh: dp: 12 (over x, z_hi), wout: 16 (over y, core), win: 4 (over z_lo).
Axes of the slice: x: 4, y: 8, z: 12 (z_hi: 3, z_lo: 4; z = z_hi * 4 + z_lo), core: 2. Of those that a mesh axis runs over, the one named last changes fastest.
Arguments:
- returned: bfloat16 [144, 256, 6144], P('dp', 'wout', 'win'), may hold values from -6 to 6
- lang_rank: int32 [48], replicated, may hold values from 0 to 11, as said below
- weight_down: bfloat16 [24576, 6144], P('wout', 'win'), may hold values from -0.078125 to 0.078125
- pre_act: bfloat16 [12288, 24576], P(('dp', 'win'), 'wout'), may hold values from -6 to 6
Outputs:
- grad_pre: bfloat16 [12288, 24576], P(('dp', 'win'), 'wout')
Inputs may be any that keep to these rules, and one draw needn't show every extreme that they name: `lang_rank`: no language rank holds more than one image of one owner (images g with the same g // 4); one language rank holds one image of every owner, so 12 slots are full there; the other ranks hold fewer and their later slots are unused.
All inputs are finite; a program needn't handle non-finite values.
Results may differ from a plain program's by a relative error of at most 0.015.
Values may be sent and summed in bfloat16 or wider, within the bound.
No kernel may reach another device: no remote copies, remote signals or barrier semaphores. Data moves between devices by JAX's collectives and lax.ppermute only.
A program may use at most 32 MiB of HBM per device.

v0:
```python
import jax
import jax.numpy as jnp
from jax import lax
from jax.sharding import PartitionSpec as P


def gelu_slope(values):
    cdf = 0.5 * (1.0 + lax.erf(values * 0.7071067811865476))
    density = jnp.exp(-0.5 * values * values) * 0.3989422804014327
    return cdf + values * density


def local(returned, lang_rank, weight_down, pre_act):
    owners = lax.axis_size("dp")
    rank_here = lax.axis_index("dp")
    images = lang_rank.shape[0]
    per_owner = images // owners
    slots = returned.shape[0]
    ranks = jnp.arange(owners, dtype=jnp.int32)
    onehot = (lang_rank[:, None] == ranks[None, :]).astype(jnp.int32)
    before = jnp.cumsum(onehot, axis=0) - onehot
    position = jnp.sum(before * onehot, axis=1).reshape(owners, per_owner)
    held_here = (lang_rank == rank_here).reshape(owners, per_owner)
    slot_ids = jnp.arange(slots, dtype=jnp.int32)
    matches = held_here[:, :, None] & (position[:, :, None] == slot_ids[None, None, :])
    select = jnp.sum(matches.astype(jnp.float32), axis=1).astype(jnp.bfloat16)
    outgoing = jnp.einsum(
        "os,spc->opc", select, returned, preferred_element_type=jnp.float32
    ).astype(jnp.bfloat16)
    incoming = lax.all_to_all(outgoing, "dp", split_axis=0, concat_axis=0, tiled=True)
    own_ranks = lax.dynamic_slice_in_dim(lang_rank, rank_here * per_owner, per_owner)
    placing = (own_ranks[:, None] == ranks[None, :]).astype(jnp.bfloat16)
    own_rows = jnp.einsum(
        "kr,rpc->kpc", placing, incoming, preferred_element_type=jnp.float32
    ).astype(jnp.bfloat16)
    gathered = lax.all_gather(own_rows, "wout", axis=1, tiled=True)
    flat_rows = gathered.reshape(-1, gathered.shape[2])
    partial_value = lax.dot_general(
        flat_rows, weight_down, (((1,), (1,)), ((), ())), preferred_element_type=jnp.float32
    )
    summed = lax.psum_scatter(
        partial_value.astype(jnp.bfloat16), "win", scatter_dimension=0, tiled=True
    ).astype(jnp.float32)
    return (summed * gelu_slope(pre_act.astype(jnp.float32))).astype(jnp.bfloat16)


def solution(mesh):
    in_specs = (P("dp", "wout", "win"), P(), P("wout", "win"), P(("dp", "win"), "wout"))
    out_specs = P(("dp", "win"), "wout")
    return jax.shard_map(local, mesh=mesh, in_specs=in_specs, out_specs=out_specs, check_vma=False)
```

profile of v0, /device:TPU:1, one launch (start us, length us, event | category | flops | bytes accessed | tf_op | source)
XLA Modules:
  0.0 185.6 jit_solution(6293368160853565514)
XLA Ops:
  6.5 0.0 copy-start
  6.5 0.8 fusion.10
  7.3 0.7 broadcast_compare_fusion
  8.0 0.1 and.10
  8.1 0.1 reduce_window_sum.11
  8.2 0.8 select_reduce_fusion
  9.0 0.1 eq.55
  9.1 0.1 convert_reduce_fusion
  9.2 0.0 copy-done
  9.2 0.5 convolution_convert_fusion.1
  9.7 0.0 copy-start.2
  9.8 1.1 copy.11
  10.9 17.0 %all-to-all-start = ((bf16[12,16,1536]{2,1,0:T(8,128)(2,1)}), bf16[12,16,1536]{2,1,0:T(8,128)(2,1)S(1)}, u32[]{:S(2)}, u32[]{:S(2)}) async-start(bf16[12,16,1536]{2,1,0:T(8,128)(2,1)} %copy.11), calls=%async_computation | async-start | bytes 1179648 | tf_op jit(solution)/shard_map/all_to_all | solution.py:30
  27.9 0.0 all-gather.2.cloned.1.call-start
  27.9 0.0 copy-done.2
  27.9 0.1 dynamic_slice.3
  28.0 19.8 %all-to-all-done = bf16[12,16,1536]{2,1,0:T(8,128)(2,1)S(1)} async-done(((bf16[12,16,1536]{2,1,0:T(8,128)(2,1)}), bf16[12,16,1536]{2,1,0:T(8,128)(2,1)S(1)}, u32[]{:S(2)}, u32[]{:S(2)}) %all-to-all-start) | async-done | bytes 589856 | tf_op jit(solution)/shard_map/all_to_all | solution.py:30
  47.8 1.1 convolution_convert_fusion.2
  48.9 0.0 all-gather.2.cloned.1.call-update
  48.9 0.0 reduce-scatter.2.cloned.1.call-start
  49.0 47.3 %all-gather.2.cloned.1.call-done = bf16[4,256,1536]{2,0,1:T(4,128)(2,1)} async-done(((bf16[4,16,1536]{2,0,1:T(4,128)(2,1)}), bf16[4,256,1536]{2,0,1:T(4,128)(2,1)}) %all-gather.2.cloned.1.call-update) | async-done | bytes 3145744 | tf_op jit(solution)/shard_map/all_gather | solution.py:36
  96.3 0.0 copy-start.3
  96.3 2.6 %copy.13 = bf16[4,256,1536]{2,1,0:T(8,128)(2,1)S(1)} copy(bf16[4,256,1536]{2,0,1:T(4,128)(2,1)} %all-gather.2.cloned.1.call-done) | data formatting | bytes 6291456 | tf_op jit(solution)/shard_map/all_gather | solution.py:36
  98.9 0.7 copy-done.3
  99.6 6.5 %convolution_convert_fusion = bf16[1024,1536]{1,0:T(8,128)(2,1)} fusion(bf16[1024,1536]{1,0:T(8,128)(2,1)S(1)} %bitcast.9, bf16[1536,1536]{1,0:T(8,128)(2,1)S(1)} %copy-done.3), kind=kOutput, calls=%fused_computation | convolution fusion | flops 4833411072 | bytes 11010048 | tf_op jit(solution)/shard_map/dot_general | solution.py:38
  106.1 0.0 copy-start.1
  106.1 0.0 reduce-scatter.2.cloned.1.call-update
  106.1 69.9 %reduce-scatter.2.cloned.1.call-done = bf16[256,1536]{1,0:T(8,128)(2,1)} async-done(((bf16[1024,1536]{1,0:T(8,128)(2,1)}), bf16[256,1536]{1,0:T(8,128)(2,1)}) %reduce-scatter.2.cloned.1.call-update) | async-done | bytes 786448 | tf_op jit(solution)/shard_map/reduce_scatter | solution.py:41
  176.0 0.0 copy-done.1
  176.0 2.7 %fusion.7 = bf16[256,1536]{1,0:T(8,128)(2,1)} fusion(bf16[256,1536]{1,0:T(8,128)(2,1)S(1)} %copy-done.1, bf16[256,1536]{1,0:T(8,128)(2,1)} %reduce-scatter.2.cloned.1.call-done), kind=kLoop, calls=%fused_computation.14 | loop fusion | flops 4718592 | bytes 2359296 | tf_op jit(solution)/shard_map/convert_element_type | solution.py:44
Async XLA Ops:
  6.5 2.7 %copy-start = (bf16[12,16,1536]{2,1,0:T(8,128)(2,1)S(1)}, bf16[12,16,1536]{2,1,0:T(8,128)(2,1)}, u32[]{:S(2)}) copy-start(bf16[12,16,1536]{2,1,0:T(8,128)(2,1)} %param.4) | copy-start | bytes 1769476
  9.7 18.2 %copy-start.2 = (s32[48]{0:T(128)S(1)}, s32[48]{0:T(128)}, u32[]{:S(2)}) copy-start(s32[48]{0:T(128)} %param.5) | copy-start | bytes 580
  10.9 36.9 %all-to-all-start = ((bf16[12,16,1536]{2,1,0:T(8,128)(2,1)}), bf16[12,16,1536]{2,1,0:T(8,128)(2,1)S(1)}, u32[]{:S(2)}, u32[]{:S(2)}) async-start(bf16[12,16,1536]{2,1,0:T(8,128)(2,1)} %copy.11), calls=%async_computation | async-start | bytes 1179648 | tf_op jit(solution)/shard_map/all_to_all | solution.py:30
  27.9 68.5 %all-gather.2.cloned.1.call-start = ((), (), s32[]{:S(2)}) async-start(), calls=%async_computation.2 | async-start | bytes 3342336 | tf_op jit(solution)/shard_map/all_gather | solution.py:36
  48.9 127.0 %reduce-scatter.2.cloned.1.call-start = ((), (), s32[]{:S(2)}) async-start(), calls=%async_computation.3 | async-start | bytes 3932160 | tf_op jit(solution)/shard_map/reduce_scatter | solution.py:41
  96.3 3.3 %copy-start.3 = (bf16[1536,1536]{1,0:T(8,128)(2,1)S(1)}, bf16[1536,1536]{1,0:T(8,128)(2,1)}, u32[]{:S(2)}) copy-start(bf16[1536,1536]{1,0:T(8,128)(2,1)} %param.6) | copy-start | bytes 14155780
  106.1 69.9 %copy-start.1 = (bf16[256,1536]{1,0:T(8,128)(2,1)S(1)}, bf16[256,1536]{1,0:T(8,128)(2,1)}, u32[]{:S(2)}) copy-start(bf16[256,1536]{1,0:T(8,128)(2,1)} %param.7) | copy-start | bytes 2359300
Sparse Core Ops, SparseCore 0:
  49.1 47.2 all-gather.1
  106.2 69.7 reduce-scatter.1
where the time goes:
time: 186 us
  waiting for transfers between devices  137 us (74%)
  starting transfers between devices  17 us (9%)
  between operations  13.5 us (7%)
  matrix products  8.13 us (4%)
  other arithmetic  5.24 us (3%)
  local copies, waits for them, and re-layouts  4.68 us (3%)
    reduce_scatter x1, waiting for transfers between devices, local(): lax.psum_scatter(partial_value.astype(jnp.bfloat16), 'win', scatter_dimen...  69.9 us
    all_gather x1, waiting for transfers between devices, local(): gathered = lax.all_gather(own_rows, 'wout', axis=1, tiled=True)  47.3 us
    all_to_all x1, waiting for transfers between devices, local(): lax.all_to_all(outgoing, 'dp', split_axis=0, concat_axis=0, tiled=True)  19.8 us
    all_to_all x1, starting transfers between devices, local(): lax.all_to_all(outgoing, 'dp', split_axis=0, concat_axis=0, tiled=True)  17 us
    dot_general x1, matrix products, local(): lax.dot_general(flat_rows, weight_down, (((1,), (1,)), ((), ())), preferr...  6.48 us
  transfers between devices with their start and end apart: 3, of which 3 were waited for; matrix products, arithmetic and copies ran while one was open for 0% of the time, Pallas kernels for 0%

commit v1 on v0

v1 whole, which is shorter than its diff:
```python
import functools

import jax
import jax.numpy as jnp
from jax import lax
from jax.experimental import pallas as pl
from jax.experimental.pallas import tpu as pltpu
from jax.sharding import PartitionSpec as P

NX, NZH, NY, NW = 4, 3, 8, 4
NZ = NZH * NW
ROWS = 16
OWNERS = NX * NZH
PER_OWNER = 4
HIDDEN_TILE = 512


def gelu_slope(values):
    cdf = 0.5 * (1.0 + lax.erf(values * 0.7071067811865476))
    density = jnp.exp(-0.5 * values * values) * 0.3989422804014327
    return cdf + values * density


def x_perm(step):
    return [(x * NZH + z, (x + step) % NX * NZH + z) for x in range(NX) for z in range(NZH)]


def zh_perm(step):
    return [(x * NZH + z, x * NZH + (z + step) % NZH) for x in range(NX) for z in range(NZH)]


def y_perm(step):
    return [(y * 2 + c, (y + step) % NY * 2 + c) for y in range(NY) for c in range(2)]


def z_perm(step):
    pairs = []
    for x in range(NX):
        for z in range(NZ):
            to = (z + step) % NZ
            pairs.append(((x * NZH + z // NW) * NW + z % NW, (x * NZH + to // NW) * NW + to % NW))
    return pairs


CORE_SWAP = [(w, w ^ 1) for w in range(2 * NY)]


def params():
    return pltpu.CompilerParams(vmem_limit_bytes=40 * 1024 * 1024)


def rank_blocks_kernel(lang_ref, returned_ref, *out_refs):
    here = lax.axis_index("dp")
    x = here // NZH
    count = jnp.int32(0)
    slots = []
    for owner in range(OWNERS):
        slot = jnp.int32(0)
        for k in range(PER_OWNER):
            hit = lang_ref[owner * PER_OWNER + k] == here
            slot = jnp.where(hit, count, slot)
            count = count + hit.astype(jnp.int32)
        slots.append(slot)
    for j in range(NX):
        to = (x + j) % NX
        for h in range(NZH):
            slot = slots[h]
            for other in range(1, NX):
                slot = jnp.where(to == other, slots[other * NZH + h], slot)
            out_refs[j][h] = returned_ref[slot]


def window_positions(z, y):
    far = jnp.where(y < NY // 2, z + 2, z + NZ - 2) % NZ
    return [far, (z + 1) % NZ, (z + NZ - 1) % NZ, z]


def window_blocks_kernel(lang_ref, *refs):
    in_refs, out_refs = refs[:NX], refs[NX:]
    here = lax.axis_index("dp")
    x, zh = here // NZH, here % NZH
    y = lax.axis_index("wout") // 2
    w = lax.axis_index("win")
    for out_ref, step in zip(out_refs, (0, 1, NZH - 1)):
        z = (zh + step) % NZH * NW + w
        for s, position in enumerate(window_positions(z, y)):
            rank = lang_ref[x * NZ + position]
            offset = (x + NX - rank // NZH) % NX
            owner = position // NW
            block = in_refs[0][owner]
            for j in range(1, NX):
                block = jnp.where(offset == j, in_refs[j][owner], block)
            out_ref[s] = block


def window_pick_kernel(lang_ref, own_ref, below_ref, above_ref, out_ref):
    here = lax.axis_index("dp")
    x, zh = here // NZH, here % NZH
    y = lax.axis_index("wout") // 2
    z = zh * NW + lax.axis_index("win")
    for s, position in enumerate(window_positions(z, y)):
        step = (zh + NZH - lang_ref[x * NZ + position] % NZH) % NZH
        block = jnp.where(step == 1, below_ref[s], own_ref[s])
        out_ref[s] = jnp.where(step == 2, above_ref[s], block)


def assemble_kernel(*refs):
    in_refs, (far_ref, near_ref, own_ref) = refs[:NY], refs[NY:]
    y = lax.axis_index("wout") // 2
    for i, ref in enumerate(in_refs):
        back = i if i <= NY // 2 else NY // 2 - i
        at = (y + NY - back) % NY
        far_ref[at] = ref[0]
        near_ref[0, at] = ref[1]
        near_ref[1, at] = ref[2]
        own_ref[at] = ref[3]


def product_kernel(splits, tiles, rows_ref, own_ref, sibling_ref, *out_refs):
    step = pl.program_id(0)

    def run(weight_ref):
        value = lax.dot_general(
            rows_ref[...], weight_ref[...], (((1,), (1,)), ((), ())), preferred_element_type=jnp.float32
        ).astype(jnp.bfloat16)
        start = 0
        for out_ref, size in zip(out_refs, splits):
            out_ref[...] = value[start:start + size]
            start += size

    @pl.when(step < tiles)
    def _():
        run(own_ref)

    @pl.when(step >= tiles)
    def _():
        run(sibling_ref)


def product(rows, own, sibling, splits):
    hidden, width = own.shape
    tiles = hidden // HIDDEN_TILE
    return pl.pallas_call(
        functools.partial(product_kernel, splits, tiles),
        grid=(2 * tiles,),
        in_specs=[
            pl.BlockSpec(rows.shape, lambda i: (0, 0)),
            pl.BlockSpec((HIDDEN_TILE, width), lambda i: (jnp.minimum(i, tiles - 1), 0)),
            pl.BlockSpec((HIDDEN_TILE, width), lambda i: (jnp.maximum(i - tiles, 0), 0)),
        ],
        out_specs=[pl.BlockSpec((size, HIDDEN_TILE), lambda i: (0, i)) for size in splits],
        out_shape=[jax.ShapeDtypeStruct((size, 2 * hidden), jnp.bfloat16) for size in splits],
        compiler_params=params(),
    )(rows, own, sibling)


def local(returned, lang_rank, weight_down, pre_act):
    core = lax.axis_index("wout") % 2
    width = returned.shape[2]
    hidden = weight_down.shape[0]
    smem = pl.BlockSpec(memory_space=pltpu.SMEM)
    vmem = pl.BlockSpec(memory_space=pltpu.VMEM)

    sibling = lax.ppermute(weight_down, "wout", CORE_SWAP)
    pre_split = pre_act.reshape(NY, 2, ROWS, hidden)
    pre_own = lax.dynamic_index_in_dim(pre_split, core, 1, keepdims=False)
    pre_sent = lax.dynamic_index_in_dim(pre_split, 1 - core, 1, keepdims=False)
    pre_sibling = lax.ppermute(pre_sent, "wout", CORE_SWAP)

    held = pl.pallas_call(
        rank_blocks_kernel,
        in_specs=[smem, vmem],
        out_specs=[vmem] * NX,
        out_shape=[jax.ShapeDtypeStruct((NZH, ROWS, width), jnp.bfloat16)] * NX,
        compiler_params=params(),
    )(lang_rank, returned)
    columns = [held[0]] + [lax.ppermute(held[j], "dp", x_perm(j)) for j in range(1, NX)]

    block4 = jax.ShapeDtypeStruct((4, ROWS, width), jnp.bfloat16)
    window_own, window_up, window_down = pl.pallas_call(
        window_blocks_kernel,
        in_specs=[smem] + [vmem] * NX,
        out_specs=[vmem] * 3,
        out_shape=[block4] * 3,
        compiler_params=params(),
    )(lang_rank, *columns)
    from_below = lax.ppermute(window_up, "dp", zh_perm(1))
    from_above = lax.ppermute(window_down, "dp", zh_perm(-1))
    window = pl.pallas_call(
        window_pick_kernel,
        in_specs=[smem] + [vmem] * 3,
        out_specs=vmem,
        out_shape=block4,
        compiler_params=params(),
    )(lang_rank, window_own, from_below, from_above)

    up, down = [window], [window]
    for step in range(4):
        up.append(lax.ppermute(up[-1], "wout", y_perm(1)))
        if step < 3:
            down.append(lax.ppermute(down[-1], "wout", y_perm(-1)))
    far, near, own = pl.pallas_call(
        assemble_kernel,
        in_specs=[vmem] * NY,
        out_specs=[vmem] * 3,
        out_shape=[
            jax.ShapeDtypeStruct((NY, ROWS, width), jnp.bfloat16),
            jax.ShapeDtypeStruct((2, NY, ROWS, width), jnp.bfloat16),
            jax.ShapeDtypeStruct((NY, ROWS, width), jnp.bfloat16),
        ],
        compiler_params=params(),
    )(*up, *down[1:])
    rows = NY * ROWS
    half = rows // 2
    far_up, far_down = product(far.reshape(rows, width), weight_down, sibling, (half, half))
    up_add, up_plain, down_plain, down_add = product(
        near.reshape(2 * rows, width), weight_down, sibling, (half,) * 4
    )
    (mine,) = product(own.reshape(rows, width), weight_down, sibling, (rows,))

    ring = ("dp", "win")
    add_up = lax.ppermute(far_up, ring, z_perm(1))
    add_down = lax.ppermute(far_down, ring, z_perm(-1))
    got_up_plain = lax.ppermute(up_plain, ring, z_perm(1))
    got_down_plain = lax.ppermute(down_plain, ring, z_perm(-1))

    def add(a, b):
        return (a.astype(jnp.float32) + b.astype(jnp.float32)).astype(jnp.bfloat16)

    got_up = lax.ppermute(add(up_add, add_up), ring, z_perm(1))
    got_down = lax.ppermute(add(down_add, add_down), ring, z_perm(-1))

    def finish(part, got_a, got_b, pre_a, pre_b):
        total = part.astype(jnp.float32) + got_a.astype(jnp.float32) + got_b.astype(jnp.float32)
        return [
            (total[:, i * hidden:(i + 1) * hidden] * gelu_slope(pre.reshape(half, hidden).astype(jnp.float32))).astype(jnp.bfloat16)
            for i, pre in enumerate((pre_a, pre_b))
        ]

    first = finish(mine[:half], got_up, got_down_plain, pre_own[:NY // 2], pre_sibling[:NY // 2])
    second = finish(mine[half:], got_up_plain, got_down, pre_own[NY // 2:], pre_sibling[NY // 2:])
    kept = jnp.concatenate([first[0], second[0]], axis=0)
    sent = jnp.concatenate([first[1], second[1]], axis=0)
    other = lax.ppermute(sent, "wout", CORE_SWAP)
    kept, other = (v.reshape(NY, 1, ROWS, hidden) for v in (kept, other))
    even = jnp.where(core == 0, kept, other)
    odd = jnp.where(core == 0, other, kept)
    return jnp.concatenate([even, odd], axis=1).reshape(2 * rows, hidden)


def solution(mesh):
    in_specs = (P("dp", "wout", "win"), P(), P("wout", "win"), P(("dp", "win"), "wout"))
    out_specs = P(("dp", "win"), "wout")
    return jax.shard_map(local, mesh=mesh, in_specs=in_specs, out_specs=out_specs, check_vma=False)
```

time: 186 us -> 158 us (0.85)
  waiting for transfers between devices: 137 us -> 36.9 us
  starting transfers between devices: 17 us -> 86.1 us
  Pallas kernels: 0 us -> 21.3 us
  between operations: 13.5 us -> 0.45 us
  matrix products: 8.13 us -> 0 us
  local copies, waits for them, and re-layouts: 4.68 us -> 9.19 us
  other arithmetic: 5.24 us -> 2.47 us
    ppermute x0 -> x21, starting transfers between devices: none -> 86.1 us  [the longest x3 13 us: local(): down.append(lax.ppermute(down[-1], 'wout', y_perm(-1)))]
    reduce_scatter x1 -> x0, waiting for transfers between devices: 69.9 us -> none  [local(): lax.psum_scatter(partial_value.astype(jnp.bfloat16), 'win', scatter_dimen...]
    all_gather x1 -> x0, waiting for transfers between devices: 47.3 us -> none  [local(): gathered = lax.all_gather(own_rows, 'wout', axis=1, tiled=True)]
    ppermute x0 -> x21, waiting for transfers between devices: none -> 36.9 us  [the longest x1 13.7 us: local(): from_above = lax.ppermute(window_down, 'dp', zh_perm(-1))]
    pallas_call x0 -> x7, Pallas kernels: none -> 21.3 us  [the longest x3 19 us: product(): pl.pallas_call(functools.partial(product_kernel, splits, tiles), grid=(2...]
    all_to_all x1 -> x0, waiting for transfers between devices: 19.8 us -> none  [local(): lax.all_to_all(outgoing, 'dp', split_axis=0, concat_axis=0, tiled=True)]
    all_to_all x1 -> x0, starting transfers between devices: 17 us -> none  [local(): lax.all_to_all(outgoing, 'dp', split_axis=0, concat_axis=0, tiled=True)]
    dot_general x3 -> x0, matrix products: 8.13 us -> none  [the longest x1 6.48 us: local(): lax.dot_general(flat_rows, weight_down, (((1,), (1,)), ((), ())), preferr...]
  transfers between devices with their start and end apart: 3 -> 21, of which waited for: 3 -> 10; matrix products, arithmetic and copies ran while one was open for 0% -> 2% of each run, Pallas kernels for 0% -> 10%
where the time goes in v1:
time: 158 us; the launch traced here: 156 us
  starting transfers between devices  86.1 us (54%)
  waiting for transfers between devices  36.9 us (23%)
  Pallas kernels  21.3 us (13%)
  local copies, waits for them, and re-layouts  9.19 us (6%)
  other arithmetic  2.47 us (2%)
    pallas_call x3, Pallas kernels, product(): pl.pallas_call(functools.partial(product_kernel, splits, tiles), grid=(2...  19 us
    ppermute x1, waiting for transfers between devices, local(): from_above = lax.ppermute(window_down, 'dp', zh_perm(-1))  13.7 us
    ppermute x3, starting transfers between devices, local(): down.append(lax.ppermute(down[-1], 'wout', y_perm(-1)))  13 us
    ppermute x1, starting transfers between devices, local(): sibling = lax.ppermute(weight_down, 'wout', CORE_SWAP)  12.4 us
    ppermute x4, waiting for transfers between devices, local(): up.append(lax.ppermute(up[-1], 'wout', y_perm(1)))  9.65 us
    ppermute x1, starting transfers between devices, local(): add_down = lax.ppermute(far_down, ring, z_perm(-1))  9.58 us
    ppermute x4, starting transfers between devices, local(): up.append(lax.ppermute(up[-1], 'wout', y_perm(1)))  8.94 us
    ppermute x3, starting transfers between devices, local(): lax.ppermute(held[j], 'dp', x_perm(j))  8.41 us
  transfers between devices with their start and end apart: 21, of which 10 were waited for; matrix products, arithmetic and copies ran while one was open for 2% of the time, Pallas kernels for 10%

profile of v1, /device:TPU:1, one launch (start us, length us, event | category | flops | bytes accessed | tf_op | source)
XLA Modules:
  0.0 156.4 jit_solution(3465845920660967952)
XLA Ops:
  0.0 12.4 %collective-permute-start.12 = (bf16[1536,1536]{1,0:T(8,128)(2,1)}, bf16[1536,1536]{1,0:T(8,128)(2,1)}, u32[]{:S(2)}, u32[]{:S(2)}) collective-permute-start(bf16[1536,1536]{1,0:T(8,128)(2,1)} %own_ref.5), channel_id=1, source_target_pairs={{0,4},{4,0},{8,12},{12,8},{16,20},{20,16},{24,28},{28,24},{32,36},... | collective-permute-start | bytes 14155784 | tf_op jit(solution)/shard_map/ppermute | solution.py:164
  12.4 1.1 copy-done.2
  13.5 0.7 copy-done.3
  14.1 0.7 shard_map.46
  14.9 1.9 %collective-permute-start = (bf16[3,16,1536]{2,1,0:T(8,128)(2,1)S(1)}, bf16[3,16,1536]{2,1,0:T(8,128)(2,1)S(1)}, u32[]{:S(2)}, u32[]{:S(2)}) collective-permute-start(bf16[3,16,1536]{2,1,0:T(8,128)(2,1)S(1)} %get-tuple-element.22), channel_id=1, source_target_pairs={{0,192},{64,256},{128,320},{192,384},{256,448},{320,512},{384,576}... | collective-permute-start | bytes 442376 | tf_op jit(solution)/shard_map/ppermute | solution.py:177
  16.8 1.9 %collective-permute-start.1 = (bf16[3,16,1536]{2,1,0:T(8,128)(2,1)S(1)}, bf16[3,16,1536]{2,1,0:T(8,128)(2,1)S(1)}, u32[]{:S(2)}, u32[]{:S(2)}) collective-permute-start(bf16[3,16,1536]{2,1,0:T(8,128)(2,1)S(1)} %get-tuple-element.23), channel_id=1, source_target_pairs={{0,384},{64,448},{128,512},{192,576},{256,640},{320,704},{384,0},{... | collective-permute-start | bytes 442376 | tf_op jit(solution)/shard_map/ppermute | solution.py:177
  18.7 4.6 %collective-permute-start.2 = (bf16[3,16,1536]{2,1,0:T(8,128)(2,1)S(1)}, bf16[3,16,1536]{2,1,0:T(8,128)(2,1)S(1)}, u32[]{:S(2)}, u32[]{:S(2)}) collective-permute-start(bf16[3,16,1536]{2,1,0:T(8,128)(2,1)S(1)} %get-tuple-element.24), channel_id=1, source_target_pairs={{0,576},{64,640},{128,704},{192,0},{256,64},{320,128},{384,192},{4... | collective-permute-start | bytes 442376 | tf_op jit(solution)/shard_map/ppermute | solution.py:177
  23.3 3.3 %collective-permute-done.refs_1_ = bf16[3,16,1536]{2,1,0:T(8,128)(2,1)S(1)} collective-permute-done((bf16[3,16,1536]{2,1,0:T(8,128)(2,1)S(1)}, bf16[3,16,1536]{2,1,0:T(8,128)(2,1)S(1)}, u32[]{:S(2)}, u32[]{:S(2)}) %collective-permute-start) | collective-permute-done | bytes 147488 | tf_op jit(solution)/shard_map/ppermute | solution.py:177
  26.6 2.2 %collective-permute-done.2.refs_3_ = bf16[3,16,1536]{2,1,0:T(8,128)(2,1)S(1)} collective-permute-done((bf16[3,16,1536]{2,1,0:T(8,128)(2,1)S(1)}, bf16[3,16,1536]{2,1,0:T(8,128)(2,1)S(1)}, u32[]{:S(2)}, u32[]{:S(2)}) %collective-permute-start.2) | collective-permute-done | bytes 147488 | tf_op jit(solution)/shard_map/ppermute | solution.py:177
  28.8 0.8 shard_map.47
  29.6 1.9 %collective-permute-start.3 = (bf16[4,16,1536]{2,1,0:T(8,128)(2,1)S(1)}, bf16[4,16,1536]{2,1,0:T(8,128)(2,1)S(1)}, u32[]{:S(2)}, u32[]{:S(2)}) collective-permute-start(bf16[4,16,1536]{2,1,0:T(8,128)(2,1)S(1)} %get-tuple-element.26), channel_id=1, source_target_pairs={{0,64},{64,128},{128,0},{192,256},{256,320},{320,192},{384,448},{4... | collective-permute-start | bytes 589832 | tf_op jit(solution)/shard_map/ppermute | solution.py:187
  31.5 7.3 %collective-permute-start.4 = (bf16[4,16,1536]{2,1,0:T(8,128)(2,1)S(1)}, bf16[4,16,1536]{2,1,0:T(8,128)(2,1)S(1)}, u32[]{:S(2)}, u32[]{:S(2)}) collective-permute-start(bf16[4,16,1536]{2,1,0:T(8,128)(2,1)S(1)} %get-tuple-element.27), channel_id=1, source_target_pairs={{0,128},{64,0},{128,64},{192,320},{256,192},{320,256},{384,512},{4... | collective-permute-start | bytes 589832 | tf_op jit(solution)/shard_map/ppermute | solution.py:188
  38.8 2.1 %collective-permute-done.3.below_ref = bf16[4,16,1536]{2,1,0:T(8,128)(2,1)S(1)} collective-permute-done((bf16[4,16,1536]{2,1,0:T(8,128)(2,1)S(1)}, bf16[4,16,1536]{2,1,0:T(8,128)(2,1)S(1)}, u32[]{:S(2)}, u32[]{:S(2)}) %collective-permute-start.3) | collective-permute-done | bytes 196640 | tf_op jit(solution)/shard_map/ppermute | solution.py:187
  40.9 13.7 %collective-permute-done.4.above_ref = bf16[4,16,1536]{2,1,0:T(8,128)(2,1)S(1)} collective-permute-done((bf16[4,16,1536]{2,1,0:T(8,128)(2,1)S(1)}, bf16[4,16,1536]{2,1,0:T(8,128)(2,1)S(1)}, u32[]{:S(2)}, u32[]{:S(2)}) %collective-permute-start.4) | collective-permute-done | bytes 196640 | tf_op jit(solution)/shard_map/ppermute | solution.py:188
  54.6 0.6 shard_map.48.refs_0_
  55.2 3.2 %collective-permute-start.5 = (bf16[4,16,1536]{2,1,0:T(8,128)(2,1)S(1)}, bf16[4,16,1536]{2,1,0:T(8,128)(2,1)S(1)}, u32[]{:S(2)}, u32[]{:S(2)}) collective-permute-start(bf16[4,16,1536]{2,1,0:T(8,128)(2,1)S(1)} %shard_map.48.refs_0_), channel_id=1, source_target_pairs={{0,8},{4,12},{8,16},{12,20},{16,24},{20,28},{24,32},{28,36},{32,40... | collective-permute-start | bytes 589832 | tf_op jit(solution)/shard_map/ppermute | solution.py:199
  58.5 3.8 %collective-permute-start.9 = (bf16[4,16,1536]{2,1,0:T(8,128)(2,1)S(1)}, bf16[4,16,1536]{2,1,0:T(8,128)(2,1)S(1)}, u32[]{:S(2)}, u32[]{:S(2)}) collective-permute-start(bf16[4,16,1536]{2,1,0:T(8,128)(2,1)S(1)} %shard_map.48.refs_0_), channel_id=1, source_target_pairs={{0,56},{4,60},{8,0},{12,4},{16,8},{20,12},{24,16},{28,20},{32,24},... | collective-permute-start | bytes 589832 | tf_op jit(solution)/shard_map/ppermute | solution.py:201
  62.3 1.8 %collective-permute-done.5.refs_1_ = bf16[4,16,1536]{2,1,0:T(8,128)(2,1)S(1)} collective-permute-done((bf16[4,16,1536]{2,1,0:T(8,128)(2,1)S(1)}, bf16[4,16,1536]{2,1,0:T(8,128)(2,1)S(1)}, u32[]{:S(2)}, u32[]{:S(2)}) %collective-permute-start.5) | collective-permute-done | bytes 196640 | tf_op jit(solution)/shard_map/ppermute | solution.py:199
  64.1 1.9 %collective-permute-start.6 = (bf16[4,16,1536]{2,1,0:T(8,128)(2,1)S(1)}, bf16[4,16,1536]{2,1,0:T(8,128)(2,1)S(1)}, u32[]{:S(2)}, u32[]{:S(2)}) collective-permute-start(bf16[4,16,1536]{2,1,0:T(8,128)(2,1)S(1)} %collective-permute-done.5.refs_1_), channel_id=1, source_target_pairs={{0,8},{4,12},{8,16},{12,20},{16,24},{20,28},{24,32},{28,36},{32,40... | collective-permute-start | bytes 589832 | tf_op jit(solution)/shard_map/ppermute | solution.py:199
  66.0 4.6 %collective-permute-start.10 = (bf16[4,16,1536]{2,1,0:T(8,128)(2,1)S(1)}, bf16[4,16,1536]{2,1,0:T(8,128)(2,1)S(1)}, u32[]{:S(2)}, u32[]{:S(2)}) collective-permute-start(bf16[4,16,1536]{2,1,0:T(8,128)(2,1)S(1)} %collective-permute-done.9.refs_5_), channel_id=1, source_target_pairs={{0,56},{4,60},{8,0},{12,4},{16,8},{20,12},{24,16},{28,20},{32,24},... | collective-permute-start | bytes 589832 | tf_op jit(solution)/shard_map/ppermute | solution.py:201
  70.6 1.1 collective-permute-done.6.refs_2_
  71.7 1.9 %collective-permute-start.7 = (bf16[4,16,1536]{2,1,0:T(8,128)(2,1)S(1)}, bf16[4,16,1536]{2,1,0:T(8,128)(2,1)S(1)}, u32[]{:S(2)}, u32[]{:S(2)}) collective-permute-start(bf16[4,16,1536]{2,1,0:T(8,128)(2,1)S(1)} %collective-permute-done.6.refs_2_), channel_id=1, source_target_pairs={{0,8},{4,12},{8,16},{12,20},{16,24},{20,28},{24,32},{28,36},{32,40... | collective-permute-start | bytes 589832 | tf_op jit(solution)/shard_map/ppermute | solution.py:199
  73.6 4.6 %collective-permute-start.11 = (bf16[4,16,1536]{2,1,0:T(8,128)(2,1)S(1)}, bf16[4,16,1536]{2,1,0:T(8,128)(2,1)S(1)}, u32[]{:S(2)}, u32[]{:S(2)}) collective-permute-start(bf16[4,16,1536]{2,1,0:T(8,128)(2,1)S(1)} %collective-permute-done.10.refs_6_), channel_id=1, source_target_pairs={{0,56},{4,60},{8,0},{12,4},{16,8},{20,12},{24,16},{28,20},{32,24},... | collective-permute-start | bytes 589832 | tf_op jit(solution)/shard_map/ppermute | solution.py:201
  78.2 1.1 collective-permute-done.7.refs_3_
  79.3 1.9 %collective-permute-start.8 = (bf16[4,16,1536]{2,1,0:T(8,128)(2,1)S(1)}, bf16[4,16,1536]{2,1,0:T(8,128)(2,1)S(1)}, u32[]{:S(2)}, u32[]{:S(2)}) collective-permute-start(bf16[4,16,1536]{2,1,0:T(8,128)(2,1)S(1)} %collective-permute-done.7.refs_3_), channel_id=1, source_target_pairs={{0,8},{4,12},{8,16},{12,20},{16,24},{20,28},{24,32},{28,36},{32,40... | collective-permute-start | bytes 589832 | tf_op jit(solution)/shard_map/ppermute | solution.py:199
  81.2 5.7 %collective-permute-done.8.refs_4_ = bf16[4,16,1536]{2,1,0:T(8,128)(2,1)S(1)} collective-permute-done((bf16[4,16,1536]{2,1,0:T(8,128)(2,1)S(1)}, bf16[4,16,1536]{2,1,0:T(8,128)(2,1)S(1)}, u32[]{:S(2)}, u32[]{:S(2)}) %collective-permute-start.8) | collective-permute-done | bytes 196640 | tf_op jit(solution)/shard_map/ppermute | solution.py:199
  86.9 0.2 shard_map.49
  87.1 2.3 %copy-done = bf16[1536,1536]{1,0:T(8,128)(2,1)S(1)} copy-done((bf16[1536,1536]{1,0:T(8,128)(2,1)S(1)}, bf16[1536,1536]{1,0:T(8,128)(2,1)}, u32[]{:S(2)}) %copy-start) | copy-done | bytes 4718616
  89.4 6.4 %shard_map.52 = (bf16[64,3072]{1,0:T(8,128)(2,1)S(1)}, bf16[64,3072]{1,0:T(8,128)(2,1)S(1)}) custom-call(bf16[128,1536]{1,0:T(8,128)(2,1)S(1)} %bitcast.29, bf16[1536,1536]{1,0:T(8,128)(2,1)S(1)} %copy-done, bf16[1536,1536]{1,0:T(8,128)(2,1)} %collective-permute-done.12.sibling_ref), custom_call_target="tpu_custom_call" | custom-call | tf_op jit(solution)/shard_map/pallas_call | solution.py:143
  95.8 9.6 %collective-permute-start.17 = (bf16[64,3072]{1,0:T(8,128)(2,1)S(1)}, bf16[64,3072]{1,0:T(8,128)(2,1)}, u32[]{:S(2)}, u32[]{:S(2)}) collective-permute-start(bf16[64,3072]{1,0:T(8,128)(2,1)S(1)} %get-tuple-element.36), channel_id=1, source_target_pairs={{0,131},{1,0},{2,1},{3,2},{64,3},{65,64},{66,65},{67,66},{128,67},... | collective-permute-start | bytes 1179656 | tf_op jit(solution)/shard_map/ppermute | solution.py:223
  105.4 0.8 dynamic-slice_bitcast_fusion
  106.2 6.4 %collective-permute-start.19 = (bf16[8,16,1536]{2,1,0:T(8,128)(2,1)}, bf16[8,16,1536]{2,1,0:T(8,128)(2,1)}, u32[]{:S(2)}, u32[]{:S(2)}) collective-permute-start(bf16[8,16,1536]{2,1,0:T(8,128)(2,1)} %dynamic-slice_bitcast_fusion), channel_id=1, source_target_pairs={{0,4},{4,0},{8,12},{12,8},{16,20},{20,16},{24,28},{28,24},{32,36},... | collective-permute-start | bytes 1179656 | tf_op jit(solution)/shard_map/ppermute | solution.py:168
  112.7 1.9 %collective-permute-start.13 = (bf16[64,3072]{1,0:T(8,128)(2,1)S(1)}, bf16[64,3072]{1,0:T(8,128)(2,1)S(1)}, u32[]{:S(2)}, u32[]{:S(2)}) collective-permute-start(bf16[64,3072]{1,0:T(8,128)(2,1)S(1)} %get-tuple-element.32), channel_id=1, source_target_pairs={{0,1},{1,2},{2,3},{3,64},{64,65},{65,66},{66,67},{67,128},{128,129... | collective-permute-start | bytes 1179656 | tf_op jit(solution)/shard_map/ppermute | solution.py:222
  114.6 2.3 %copy-done.1 = bf16[1536,1536]{1,0:T(8,128)(2,1)S(1)} copy-done((bf16[1536,1536]{1,0:T(8,128)(2,1)S(1)}, bf16[1536,1536]{1,0:T(8,128)(2,1)}, u32[]{:S(2)}) %copy-start.1) | copy-done | bytes 4718616
  117.0 6.3 %shard_map.51 = (bf16[64,3072]{1,0:T(8,128)(2,1)S(1)}, bf16[64,3072]{1,0:T(8,128)(2,1)S(1)}, bf16[64,3072]{1,0:T(8,128)(2,1)S(1)}, bf16[64,3072]{1,0:T(8,128)(2,1)S(1)}) custom-call(bf16[256,1536]{1,0:T(8,128)(2,1)S(1)} %bitcast.28, bf16[1536,1536]{1,0:T(8,128)(2,1)S(1)} %copy-done.1, bf16[1536,1536]{1,0:T(8,128)(2,1)} %collective-permute-done.12.sibling_ref), custom_call_target="tpu_custom_call" | custom-call | tf_op jit(solution)/shard_map/pallas_call | solution.py:143
  123.3 4.6 %collective-permute-start.15 = (bf16[64,3072]{1,0:T(8,128)(2,1)S(1)}, bf16[64,3072]{1,0:T(8,128)(2,1)S(1)}, u32[]{:S(2)}, u32[]{:S(2)}) collective-permute-start(bf16[64,3072]{1,0:T(8,128)(2,1)S(1)} %get-tuple-element.33), channel_id=1, source_target_pairs={{0,131},{1,0},{2,1},{3,2},{64,3},{65,64},{66,65},{67,66},{128,67},... | collective-permute-start | bytes 1179656 | tf_op jit(solution)/shard_map/ppermute | solution.py:225
  127.9 1.9 %collective-permute-start.16 = (bf16[64,3072]{1,0:T(8,128)(2,1)S(1)}, bf16[64,3072]{1,0:T(8,128)(2,1)S(1)}, u32[]{:S(2)}, u32[]{:S(2)}) collective-permute-start(bf16[64,3072]{1,0:T(8,128)(2,1)S(1)} %get-tuple-element.34), channel_id=1, source_target_pairs={{0,1},{1,2},{2,3},{3,64},{64,65},{65,66},{66,67},{67,128},{128,129... | collective-permute-start | bytes 1179656 | tf_op jit(solution)/shard_map/ppermute | solution.py:224
  129.8 1.1 add_convert_fusion
  130.9 4.6 %collective-permute-start.18 = (bf16[64,3072]{1,0:T(8,128)(2,1)S(1)}, bf16[64,3072]{1,0:T(8,128)(2,1)S(1)}, u32[]{:S(2)}, u32[]{:S(2)}) collective-permute-start(bf16[64,3072]{1,0:T(8,128)(2,1)S(1)} %add_convert_fusion), channel_id=1, source_target_pairs={{0,131},{1,0},{2,1},{3,2},{64,3},{65,64},{66,65},{67,66},{128,67},... | collective-permute-start | bytes 1179656 | tf_op jit(solution)/shard_map/ppermute | solution.py:231
  135.6 1.9 %collective-permute-start.14 = (bf16[64,3072]{1,0:T(8,128)(2,1)S(1)}, bf16[64,3072]{1,0:T(8,128)(2,1)S(1)}, u32[]{:S(2)}, u32[]{:S(2)}) collective-permute-start(bf16[64,3072]{1,0:T(8,128)(2,1)S(1)} %add_convert_fusion.1), channel_id=1, source_target_pairs={{0,1},{1,2},{2,3},{3,64},{64,65},{65,66},{66,67},{67,128},{128,129... | collective-permute-start | bytes 1179656 | tf_op jit(solution)/shard_map/ppermute | solution.py:230
  137.5 1.0 fusion.32
  138.6 6.3 %shard_map.50 = bf16[128,3072]{1,0:T(8,128)(2,1)S(1)} custom-call(bf16[128,1536]{1,0:T(8,128)(2,1)S(1)} %bitcast.30, bf16[1536,1536]{1,0:T(8,128)(2,1)S(1)} %bitcast.27, bf16[1536,1536]{1,0:T(8,128)(2,1)} %collective-permute-done.12.sibling_ref), custom_call_target="tpu_custom_call" | custom-call | tf_op jit(solution)/shard_map/pallas_call | solution.py:143
  145.0 4.6 %collective-permute-done.14 = bf16[64,3072]{1,0:T(8,128)(2,1)S(1)} collective-permute-done((bf16[64,3072]{1,0:T(8,128)(2,1)S(1)}, bf16[64,3072]{1,0:T(8,128)(2,1)S(1)}, u32[]{:S(2)}, u32[]{:S(2)}) %collective-permute-start.14) | collective-permute-done | bytes 393248 | tf_op jit(solution)/shard_map/ppermute | solution.py:230
  149.6 0.3 convert_add_fusion.1
  149.9 0.7 fusion.30
  150.7 3.3 %collective-permute-start.20 = (bf16[128,1536]{1,0:T(8,128)(2,1)S(1)}, bf16[128,1536]{1,0:T(8,128)(2,1)S(1)}, u32[]{:S(2)}, u32[]{:S(2)}) collective-permute-start(bf16[128,1536]{1,0:T(8,128)(2,1)S(1)} %pad_maximum_fusion.2), channel_id=1, source_target_pairs={{0,4},{4,0},{8,12},{12,8},{16,20},{20,16},{24,28},{28,24},{32,36},... | collective-permute-start | bytes 1179656 | tf_op jit(solution)/shard_map/ppermute | solution.py:244
  154.0 1.3 collective-permute-done.20
  155.5 0.9 copy.6
  (27 shorter events, 0.4 us)
Async XLA Ops:
  0.0 87.1 %collective-permute-start.12 = (bf16[1536,1536]{1,0:T(8,128)(2,1)}, bf16[1536,1536]{1,0:T(8,128)(2,1)}, u32[]{:S(2)}, u32[]{:S(2)}) collective-permute-start(bf16[1536,1536]{1,0:T(8,128)(2,1)} %own_ref.5), channel_id=1, source_target_pairs={{0,4},{4,0},{8,12},{12,8},{16,20},{20,16},{24,28},{28,24},{32,36},... | collective-permute-start | bytes 14155784 | tf_op jit(solution)/shard_map/ppermute | solution.py:164
  12.4 1.1 copy-start.2
  13.5 0.7 copy-start.3
  14.9 11.7 %collective-permute-start = (bf16[3,16,1536]{2,1,0:T(8,128)(2,1)S(1)}, bf16[3,16,1536]{2,1,0:T(8,128)(2,1)S(1)}, u32[]{:S(2)}, u32[]{:S(2)}) collective-permute-start(bf16[3,16,1536]{2,1,0:T(8,128)(2,1)S(1)} %get-tuple-element.22), channel_id=1, source_target_pairs={{0,192},{64,256},{128,320},{192,384},{256,448},{320,512},{384,576}... | collective-permute-start | bytes 442376 | tf_op jit(solution)/shard_map/ppermute | solution.py:177
  16.8 9.8 %collective-permute-start.1 = (bf16[3,16,1536]{2,1,0:T(8,128)(2,1)S(1)}, bf16[3,16,1536]{2,1,0:T(8,128)(2,1)S(1)}, u32[]{:S(2)}, u32[]{:S(2)}) collective-permute-start(bf16[3,16,1536]{2,1,0:T(8,128)(2,1)S(1)} %get-tuple-element.23), channel_id=1, source_target_pairs={{0,384},{64,448},{128,512},{192,576},{256,640},{320,704},{384,0},{... | collective-permute-start | bytes 442376 | tf_op jit(solution)/shard_map/ppermute | solution.py:177
  18.7 10.1 %collective-permute-start.2 = (bf16[3,16,1536]{2,1,0:T(8,128)(2,1)S(1)}, bf16[3,16,1536]{2,1,0:T(8,128)(2,1)S(1)}, u32[]{:S(2)}, u32[]{:S(2)}) collective-permute-start(bf16[3,16,1536]{2,1,0:T(8,128)(2,1)S(1)} %get-tuple-element.24), channel_id=1, source_target_pairs={{0,576},{64,640},{128,704},{192,0},{256,64},{320,128},{384,192},{4... | collective-permute-start | bytes 442376 | tf_op jit(solution)/shard_map/ppermute | solution.py:177
  29.6 11.3 %collective-permute-start.3 = (bf16[4,16,1536]{2,1,0:T(8,128)(2,1)S(1)}, bf16[4,16,1536]{2,1,0:T(8,128)(2,1)S(1)}, u32[]{:S(2)}, u32[]{:S(2)}) collective-permute-start(bf16[4,16,1536]{2,1,0:T(8,128)(2,1)S(1)} %get-tuple-element.26), channel_id=1, source_target_pairs={{0,64},{64,128},{128,0},{192,256},{256,320},{320,192},{384,448},{4... | collective-permute-start | bytes 589832 | tf_op jit(solution)/shard_map/ppermute | solution.py:187
  31.5 23.0 %collective-permute-start.4 = (bf16[4,16,1536]{2,1,0:T(8,128)(2,1)S(1)}, bf16[4,16,1536]{2,1,0:T(8,128)(2,1)S(1)}, u32[]{:S(2)}, u32[]{:S(2)}) collective-permute-start(bf16[4,16,1536]{2,1,0:T(8,128)(2,1)S(1)} %get-tuple-element.27), channel_id=1, source_target_pairs={{0,128},{64,0},{128,64},{192,320},{256,192},{320,256},{384,512},{4... | collective-permute-start | bytes 589832 | tf_op jit(solution)/shard_map/ppermute | solution.py:188
  55.2 8.8 %collective-permute-start.5 = (bf16[4,16,1536]{2,1,0:T(8,128)(2,1)S(1)}, bf16[4,16,1536]{2,1,0:T(8,128)(2,1)S(1)}, u32[]{:S(2)}, u32[]{:S(2)}) collective-permute-start(bf16[4,16,1536]{2,1,0:T(8,128)(2,1)S(1)} %shard_map.48.refs_0_), channel_id=1, source_target_pairs={{0,8},{4,12},{8,16},{12,20},{16,24},{20,28},{24,32},{28,36},{32,40... | collective-permute-start | bytes 589832 | tf_op jit(solution)/shard_map/ppermute | solution.py:199
  58.5 7.5 %collective-permute-start.9 = (bf16[4,16,1536]{2,1,0:T(8,128)(2,1)S(1)}, bf16[4,16,1536]{2,1,0:T(8,128)(2,1)S(1)}, u32[]{:S(2)}, u32[]{:S(2)}) collective-permute-start(bf16[4,16,1536]{2,1,0:T(8,128)(2,1)S(1)} %shard_map.48.refs_0_), channel_id=1, source_target_pairs={{0,56},{4,60},{8,0},{12,4},{16,8},{20,12},{24,16},{28,20},{32,24},... | collective-permute-start | bytes 589832 | tf_op jit(solution)/shard_map/ppermute | solution.py:201
  64.1 7.6 %collective-permute-start.6 = (bf16[4,16,1536]{2,1,0:T(8,128)(2,1)S(1)}, bf16[4,16,1536]{2,1,0:T(8,128)(2,1)S(1)}, u32[]{:S(2)}, u32[]{:S(2)}) collective-permute-start(bf16[4,16,1536]{2,1,0:T(8,128)(2,1)S(1)} %collective-permute-done.5.refs_1_), channel_id=1, source_target_pairs={{0,8},{4,12},{8,16},{12,20},{16,24},{20,28},{24,32},{28,36},{32,40... | collective-permute-start | bytes 589832 | tf_op jit(solution)/shard_map/ppermute | solution.py:199
  66.0 7.6 %collective-permute-start.10 = (bf16[4,16,1536]{2,1,0:T(8,128)(2,1)S(1)}, bf16[4,16,1536]{2,1,0:T(8,128)(2,1)S(1)}, u32[]{:S(2)}, u32[]{:S(2)}) collective-permute-start(bf16[4,16,1536]{2,1,0:T(8,128)(2,1)S(1)} %collective-permute-done.9.refs_5_), channel_id=1, source_target_pairs={{0,56},{4,60},{8,0},{12,4},{16,8},{20,12},{24,16},{28,20},{32,24},... | collective-permute-start | bytes 589832 | tf_op jit(solution)/shard_map/ppermute | solution.py:201
  71.7 7.6 %collective-permute-start.7 = (bf16[4,16,1536]{2,1,0:T(8,128)(2,1)S(1)}, bf16[4,16,1536]{2,1,0:T(8,128)(2,1)S(1)}, u32[]{:S(2)}, u32[]{:S(2)}) collective-permute-start(bf16[4,16,1536]{2,1,0:T(8,128)(2,1)S(1)} %collective-permute-done.6.refs_2_), channel_id=1, source_target_pairs={{0,8},{4,12},{8,16},{12,20},{16,24},{20,28},{24,32},{28,36},{32,40... | collective-permute-start | bytes 589832 | tf_op jit(solution)/shard_map/ppermute | solution.py:199
  73.6 7.6 %collective-permute-start.11 = (bf16[4,16,1536]{2,1,0:T(8,128)(2,1)S(1)}, bf16[4,16,1536]{2,1,0:T(8,128)(2,1)S(1)}, u32[]{:S(2)}, u32[]{:S(2)}) collective-permute-start(bf16[4,16,1536]{2,1,0:T(8,128)(2,1)S(1)} %collective-permute-done.10.refs_6_), channel_id=1, source_target_pairs={{0,56},{4,60},{8,0},{12,4},{16,8},{20,12},{24,16},{28,20},{32,24},... | collective-permute-start | bytes 589832 | tf_op jit(solution)/shard_map/ppermute | solution.py:201
  79.3 7.6 %collective-permute-start.8 = (bf16[4,16,1536]{2,1,0:T(8,128)(2,1)S(1)}, bf16[4,16,1536]{2,1,0:T(8,128)(2,1)S(1)}, u32[]{:S(2)}, u32[]{:S(2)}) collective-permute-start(bf16[4,16,1536]{2,1,0:T(8,128)(2,1)S(1)} %collective-permute-done.7.refs_3_), channel_id=1, source_target_pairs={{0,8},{4,12},{8,16},{12,20},{16,24},{20,28},{24,32},{28,36},{32,40... | collective-permute-start | bytes 589832 | tf_op jit(solution)/shard_map/ppermute | solution.py:199
  87.1 2.3 %copy-start = (bf16[1536,1536]{1,0:T(8,128)(2,1)S(1)}, bf16[1536,1536]{1,0:T(8,128)(2,1)}, u32[]{:S(2)}) copy-start(bf16[1536,1536]{1,0:T(8,128)(2,1)} %own_ref.5) | copy-start | bytes 14155780
  89.4 16.0 %copy-start.4 = (bf16[256,1536]{1,0:T(8,128)(2,1)S(1)}, bf16[256,1536]{1,0:T(8,128)(2,1)}, u32[]{:S(2)}) copy-start(bf16[256,1536]{1,0:T(8,128)(2,1)} %param.7) | copy-start | bytes 2359300
  95.8 34.0 %collective-permute-start.17 = (bf16[64,3072]{1,0:T(8,128)(2,1)S(1)}, bf16[64,3072]{1,0:T(8,128)(2,1)}, u32[]{:S(2)}, u32[]{:S(2)}) collective-permute-start(bf16[64,3072]{1,0:T(8,128)(2,1)S(1)} %get-tuple-element.36), channel_id=1, source_target_pairs={{0,131},{1,0},{2,1},{3,2},{64,3},{65,64},{66,65},{67,66},{128,67},... | collective-permute-start | bytes 1179656 | tf_op jit(solution)/shard_map/ppermute | solution.py:223
  105.4 33.2 %slice-start = ((s8[4718592]{0:T(1024)(128)(4,1)}), s8[524288]{0:T(1024)(128)(4,1)S(1)}, s32[]{:S(2)}) async-start(s8[4718592]{0:T(1024)(128)(4,1)} %bitcast.26), calls=%async_computation | async-start | bytes 1048576
  106.2 31.3 %collective-permute-start.19 = (bf16[8,16,1536]{2,1,0:T(8,128)(2,1)}, bf16[8,16,1536]{2,1,0:T(8,128)(2,1)}, u32[]{:S(2)}, u32[]{:S(2)}) collective-permute-start(bf16[8,16,1536]{2,1,0:T(8,128)(2,1)} %dynamic-slice_bitcast_fusion), channel_id=1, source_target_pairs={{0,4},{4,0},{8,12},{12,8},{16,20},{20,16},{24,28},{28,24},{32,36},... | collective-permute-start | bytes 1179656 | tf_op jit(solution)/shard_map/ppermute | solution.py:168
  112.7 22.8 %collective-permute-start.13 = (bf16[64,3072]{1,0:T(8,128)(2,1)S(1)}, bf16[64,3072]{1,0:T(8,128)(2,1)S(1)}, u32[]{:S(2)}, u32[]{:S(2)}) collective-permute-start(bf16[64,3072]{1,0:T(8,128)(2,1)S(1)} %get-tuple-element.32), channel_id=1, source_target_pairs={{0,1},{1,2},{2,3},{3,64},{64,65},{65,66},{66,67},{67,128},{128,129... | collective-permute-start | bytes 1179656 | tf_op jit(solution)/shard_map/ppermute | solution.py:222
  114.6 2.3 %copy-start.1 = (bf16[1536,1536]{1,0:T(8,128)(2,1)S(1)}, bf16[1536,1536]{1,0:T(8,128)(2,1)}, u32[]{:S(2)}) copy-start(bf16[1536,1536]{1,0:T(8,128)(2,1)} %own_ref.5) | copy-start | bytes 14155780
  117.0 21.6 %slice-start.1 = ((s8[4718592]{0:T(1024)(128)(4,1)}), s8[4194304]{0:T(1024)(128)(4,1)S(1)}, s32[]{:S(2)}) async-start(s8[4718592]{0:T(1024)(128)(4,1)} %bitcast.26), calls=%async_computation.1 | async-start | bytes 8388608
  123.3 21.6 %collective-permute-start.15 = (bf16[64,3072]{1,0:T(8,128)(2,1)S(1)}, bf16[64,3072]{1,0:T(8,128)(2,1)S(1)}, u32[]{:S(2)}, u32[]{:S(2)}) collective-permute-start(bf16[64,3072]{1,0:T(8,128)(2,1)S(1)} %get-tuple-element.33), channel_id=1, source_target_pairs={{0,131},{1,0},{2,1},{3,2},{64,3},{65,64},{66,65},{67,66},{128,67},... | collective-permute-start | bytes 1179656 | tf_op jit(solution)/shard_map/ppermute | solution.py:225
  127.9 17.1 %collective-permute-start.16 = (bf16[64,3072]{1,0:T(8,128)(2,1)S(1)}, bf16[64,3072]{1,0:T(8,128)(2,1)S(1)}, u32[]{:S(2)}, u32[]{:S(2)}) collective-permute-start(bf16[64,3072]{1,0:T(8,128)(2,1)S(1)} %get-tuple-element.34), channel_id=1, source_target_pairs={{0,1},{1,2},{2,3},{3,64},{64,65},{65,66},{66,67},{67,128},{128,129... | collective-permute-start | bytes 1179656 | tf_op jit(solution)/shard_map/ppermute | solution.py:224
  130.9 14.0 %collective-permute-start.18 = (bf16[64,3072]{1,0:T(8,128)(2,1)S(1)}, bf16[64,3072]{1,0:T(8,128)(2,1)S(1)}, u32[]{:S(2)}, u32[]{:S(2)}) collective-permute-start(bf16[64,3072]{1,0:T(8,128)(2,1)S(1)} %add_convert_fusion), channel_id=1, source_target_pairs={{0,131},{1,0},{2,1},{3,2},{64,3},{65,64},{66,65},{67,66},{128,67},... | collective-permute-start | bytes 1179656 | tf_op jit(solution)/shard_map/ppermute | solution.py:231
  135.6 14.0 %collective-permute-start.14 = (bf16[64,3072]{1,0:T(8,128)(2,1)S(1)}, bf16[64,3072]{1,0:T(8,128)(2,1)S(1)}, u32[]{:S(2)}, u32[]{:S(2)}) collective-permute-start(bf16[64,3072]{1,0:T(8,128)(2,1)S(1)} %add_convert_fusion.1), channel_id=1, source_target_pairs={{0,1},{1,2},{2,3},{3,64},{64,65},{65,66},{66,67},{67,128},{128,129... | collective-permute-start | bytes 1179656 | tf_op jit(solution)/shard_map/ppermute | solution.py:230
  150.7 4.6 %collective-permute-start.20 = (bf16[128,1536]{1,0:T(8,128)(2,1)S(1)}, bf16[128,1536]{1,0:T(8,128)(2,1)S(1)}, u32[]{:S(2)}, u32[]{:S(2)}) collective-permute-start(bf16[128,1536]{1,0:T(8,128)(2,1)S(1)} %pad_maximum_fusion.2), channel_id=1, source_target_pairs={{0,4},{4,0},{8,12},{12,8},{16,20},{20,16},{24,28},{28,24},{32,36},... | collective-permute-start | bytes 1179656 | tf_op jit(solution)/shard_map/ppermute | solution.py:244

commit v2 on v0

v2 whole, which is shorter than its diff:
```python
import functools

import jax
import jax.numpy as jnp
from jax import lax
from jax.experimental import pallas as pl
from jax.experimental.pallas import tpu as pltpu
from jax.sharding import PartitionSpec as P

NX, NZH, NY, NW = 4, 3, 8, 4
NZ = NZH * NW
ROWS = 16
OWNERS = NX * NZH
PER_OWNER = 4
SLOTS = 4
HALF = NY // 2
HIDDEN_TILE = 768

X_GROUPS = [[x * NZH + z for x in range(NX)] for z in range(NZH)]
PARITY_GROUPS = [[y * 2 + c for y in range(p, NY, 2)] for p in range(2) for c in range(2)]
CORE_SWAP = [(w, w ^ 1) for w in range(2 * NY)]
RING = ("dp", "wout", "win")


def gelu_slope(values):
    cdf = 0.5 * (1.0 + lax.erf(values * 0.7071067811865476))
    density = jnp.exp(-0.5 * values * values) * 0.3989422804014327
    return cdf + values * density


def ring_perm(step):
    def index(x, z, w):
        return ((x * NZH + z // NW) * 2 * NY + w) * NW + z % NW

    return [
        (index(x, z, w), index(x, (z + (step if w % 2 == 0 else -step)) % NZ, w))
        for x in range(NX) for z in range(NZ) for w in range(2 * NY)
    ]


def zh_perm(step):
    return [(x * NZH + z, x * NZH + (z + step) % NZH) for x in range(NX) for z in range(NZH)]


def y_perm(step):
    return [(y * 2 + c, (y + step) % NY * 2 + c) for y in range(NY) for c in range(2)]


def params():
    return pltpu.CompilerParams(vmem_limit_bytes=40 * 1024 * 1024)


def rank_blocks_kernel(lang_ref, returned_ref, out_ref):
    here = lax.axis_index("dp")
    count = jnp.int32(0)
    for owner in range(OWNERS):
        slot = jnp.int32(0)
        for k in range(PER_OWNER):
            hit = lang_ref[owner * PER_OWNER + k] == here
            slot = jnp.where(hit, count, slot)
            count = count + hit.astype(jnp.int32)
        out_ref[owner // NZH, owner % NZH * ROWS:(owner % NZH + 1) * ROWS] = returned_ref[slot]


def window_positions(z, core):
    sign = 1 - 2 * core
    return [(z + NZ + sign * step) % NZ for step in (2, 1, -1, 0)]


def window_blocks_kernel(lang_ref, in_ref, *out_refs):
    here = lax.axis_index("dp")
    column = here // NZH
    core = lax.axis_index("wout") % 2
    w = lax.axis_index("win")
    for h in range(NZH):
        for s, position in enumerate(window_positions((here + h) % NZH * NW + w, core)):
            rank = lang_ref[column * NZ + position]
            start = pl.multiple_of(position // NW * ROWS, ROWS)
            out_refs[h][s * ROWS:(s + 1) * ROWS] = in_ref[rank // NZH, pl.ds(start, ROWS)]


def window_pick_kernel(lang_ref, *refs):
    in_refs, out_ref = refs[:NZH], refs[NZH]
    here = lax.axis_index("dp")
    core = lax.axis_index("wout") % 2
    z = here % NZH * NW + lax.axis_index("win")
    for s, position in enumerate(window_positions(z, core)):
        rows = slice(s * ROWS, (s + 1) * ROWS)
        back = (here + NZH - lang_ref[here // NZH * NZ + position] % NZH) % NZH
        block = in_refs[0][rows]
        for j in range(1, NZH):
            block = jnp.where(back == j, in_refs[j][rows], block)
        out_ref[rows] = block


def product_kernel(count, *refs):
    rows_refs, (sibling_ref, own_hbm), out_refs = refs[:count], refs[count:count + 2], refs[count + 2:-2]
    own_ref, sem = refs[-2:]
    copy = pltpu.make_async_copy(own_hbm, own_ref, sem)
    copy.start()
    hidden, width = sibling_ref.shape
    rows = jnp.concatenate(
        [
            ref[:, s * ROWS:(s + 1) * ROWS].reshape(-1, width)
            for s in range(SLOTS) for ref in rows_refs
        ],
        axis=0,
    )

    def run(weight_ref, start):
        for tile in range(0, hidden, HIDDEN_TILE):
            value = lax.dot_general(
                rows, weight_ref[tile:tile + HIDDEN_TILE], (((1,), (1,)), ((), ())),
                preferred_element_type=jnp.float32,
            ).astype(jnp.bfloat16)
            for s, out_ref in enumerate(out_refs):
                size = out_ref.shape[0]
                out_ref[:, start + tile:start + tile + HIDDEN_TILE] = value[s * size:(s + 1) * size]

    run(sibling_ref, hidden)
    copy.wait()
    run(own_ref, 0)


def product(blocks, own, sibling):
    hidden, width = own.shape
    vmem = pl.BlockSpec(memory_space=pltpu.VMEM)
    return pl.pallas_call(
        functools.partial(product_kernel, len(blocks)),
        in_specs=[vmem] * (len(blocks) + 1) + [pl.BlockSpec(memory_space=pl.ANY)],
        out_specs=[vmem] * SLOTS,
        out_shape=[jax.ShapeDtypeStruct((HALF * ROWS, 2 * hidden), jnp.bfloat16)] * SLOTS,
        scratch_shapes=[pltpu.VMEM((hidden, width), jnp.bfloat16), pltpu.SemaphoreType.DMA],
        compiler_params=params(),
    )(*blocks, sibling, own)


def parity_and_core():
    place = lax.axis_index("wout")
    return place // 2 % 2, place % 2


def split_kernel(pre_ref, kept_ref, sent_ref):
    parity, core = parity_and_core()
    for h in range(2):
        for j in range(HALF):
            kept_ref[h, j] = pre_ref[j, (parity + h) % 2, core]
            sent_ref[h, j] = pre_ref[j, (parity + h) % 2, 1 - core]


def finish_kernel(*refs):
    parts, (pre_own, pre_sibling, kept_ref, sent_ref) = refs[:6], refs[6:]
    hidden = pre_own.shape[3]
    for h in range(2):
        mine, ahead, behind = parts[3 * h:3 * h + 3]
        for i, (pre_ref, out_ref) in enumerate(((pre_own, kept_ref), (pre_sibling, sent_ref))):
            for j in range(HALF):
                at = slice(j * ROWS, (j + 1) * ROWS), slice(i * hidden, (i + 1) * hidden)
                total = mine[at].astype(jnp.float32) + ahead[at].astype(jnp.float32) + behind[at].astype(jnp.float32)
                out_ref[h, j] = (total * gelu_slope(pre_ref[h, j].astype(jnp.float32))).astype(jnp.bfloat16)


def join_kernel(kept_ref, other_ref, out_ref):
    parity, core = parity_and_core()
    for h in range(2):
        for j in range(HALF):
            out_ref[j, (parity + h) % 2, core] = kept_ref[h, j]
            out_ref[j, (parity + h) % 2, 1 - core] = other_ref[h, j]


def local(returned, lang_rank, weight_down, pre_act):
    width = returned.shape[2]
    hidden = weight_down.shape[0]
    smem = pl.BlockSpec(memory_space=pltpu.SMEM)
    vmem = pl.BlockSpec(memory_space=pltpu.VMEM)

    def move(kernel, out, *values, count=None):
        shape = jax.ShapeDtypeStruct(out + (width,), jnp.bfloat16)
        return pl.pallas_call(
            kernel,
            in_specs=[smem] + [vmem] * len(values),
            out_specs=vmem if count is None else [vmem] * count,
            out_shape=shape if count is None else [shape] * count,
            compiler_params=params(),
        )(lang_rank, *values)

    held = move(rank_blocks_kernel, (NX, NZH * ROWS), returned)
    held = lax.all_to_all(held, "dp", 0, 0, axis_index_groups=X_GROUPS)
    windows = move(window_blocks_kernel, (SLOTS * ROWS,), held, count=NZH)
    weight_down, pre_act, _ = lax.optimization_barrier((weight_down, pre_act, windows[1]))
    sibling = lax.ppermute(weight_down, "wout", CORE_SWAP)
    halves = jax.ShapeDtypeStruct((2, HALF, ROWS, hidden), jnp.bfloat16)
    pre_own, pre_sent = pl.pallas_call(
        split_kernel,
        in_specs=[vmem],
        out_specs=[vmem] * 2,
        out_shape=[halves] * 2,
        compiler_params=params(),
    )(pre_act.reshape(HALF, 2, 2, ROWS, hidden))
    pre_sibling = lax.ppermute(pre_sent, "wout", CORE_SWAP)
    windows = [windows[0]] + [lax.ppermute(windows[j], "dp", zh_perm(j)) for j in range(1, NZH)]
    window = move(window_pick_kernel, (SLOTS * ROWS,), *windows)
    near = lax.all_gather(window, "wout", axis_index_groups=PARITY_GROUPS)
    others = [
        lax.ppermute(near[:HALF // 2], "wout", y_perm(1)),
        lax.ppermute(near[HALF // 2:], "wout", y_perm(-1)),
    ]

    parts = []
    for blocks in ([near], others):
        far, ahead, behind, mine = product(blocks, weight_down, sibling)
        far = lax.ppermute(far, RING, ring_perm(1))
        behind = lax.ppermute(behind, RING, ring_perm(-1))
        ahead = (ahead.astype(jnp.float32) + far.astype(jnp.float32)).astype(jnp.bfloat16)
        parts += [mine, lax.ppermute(ahead, RING, ring_perm(1)), behind]

    kept, sent = pl.pallas_call(
        finish_kernel,
        in_specs=[vmem] * 8,
        out_specs=[vmem] * 2,
        out_shape=[halves] * 2,
        compiler_params=params(),
    )(*parts, pre_own, pre_sibling)
    other = lax.ppermute(sent, "wout", CORE_SWAP)
    out = pl.pallas_call(
        join_kernel,
        in_specs=[vmem] * 2,
        out_specs=vmem,
        out_shape=jax.ShapeDtypeStruct((HALF, 2, 2, ROWS, hidden), jnp.bfloat16),
        compiler_params=params(),
    )(kept, other)
    return out.reshape(2 * NY * ROWS, hidden)


def solution(mesh):
    in_specs = (P("dp", "wout", "win"), P(), P("wout", "win"), P(("dp", "win"), "wout"))
    out_specs = P(("dp", "win"), "wout")
    return jax.shard_map(local, mesh=mesh, in_specs=in_specs, out_specs=out_specs, check_vma=False)
```

time: 186 us -> 135 us (0.73)
  waiting for transfers between devices: 137 us -> 30.7 us
  starting transfers between devices: 17 us -> 60.4 us
  blocking collectives: 0 us -> 30.2 us
  between operations: 13.5 us -> 0.25 us
  Pallas kernels: 0 us -> 10.4 us
  matrix products: 8.13 us -> 0 us
  other arithmetic: 5.24 us -> 0.19 us
  local copies, waits for them, and re-layouts: 4.68 us -> 2.22 us
    reduce_scatter x1 -> x0, waiting for transfers between devices: 69.9 us -> none  [local(): lax.psum_scatter(partial_value.astype(jnp.bfloat16), 'win', scatter_dimen...]
    ppermute x0 -> x13, starting transfers between devices: none -> 60.4 us  [the longest x2 13.9 us: local(): far = lax.ppermute(far, RING, ring_perm(1))]
    all_gather x1 -> x0, waiting for transfers between devices: 47.3 us -> none  [local(): gathered = lax.all_gather(own_rows, 'wout', axis=1, tiled=True)]
    ppermute x0 -> x13, waiting for transfers between devices: none -> 30.7 us  [the longest x2 18.2 us: local(): lax.ppermute(windows[j], 'dp', zh_perm(j))]
    all_to_all x1 -> x0, waiting for transfers between devices: 19.8 us -> none  [local(): lax.all_to_all(outgoing, 'dp', split_axis=0, concat_axis=0, tiled=True)]
    all_gather x0 -> x1, blocking collectives: none -> 18.3 us  [local(): near = lax.all_gather(window, 'wout', axis_index_groups=PARITY_GROUPS)]
    all_to_all x1 -> x0, starting transfers between devices: 17 us -> none  [local(): lax.all_to_all(outgoing, 'dp', split_axis=0, concat_axis=0, tiled=True)]
    all_to_all x0 -> x1, blocking collectives: none -> 11.9 us  [local(): held = lax.all_to_all(held, 'dp', 0, 0, axis_index_groups=X_GROUPS)]
  transfers between devices with their start and end apart: 3 -> 13, of which waited for: 3 -> 7; matrix products, arithmetic and copies ran while one was open for 0% -> 0% of each run, Pallas kernels for 0% -> 5%
where the time goes in v2:
time: 135 us; the launch traced here: 134 us
  starting transfers between devices  60.4 us (45%)
  waiting for transfers between devices  30.7 us (23%)
  blocking collectives  30.2 us (22%)
  Pallas kernels  10.4 us (8%)
  local copies, waits for them, and re-layouts  2.22 us (2%)
    all_gather x1, blocking collectives, local(): near = lax.all_gather(window, 'wout', axis_index_groups=PARITY_GROUPS)  18.3 us
    ppermute x2, waiting for transfers between devices, local(): lax.ppermute(windows[j], 'dp', zh_perm(j))  18.2 us
    ppermute x2, starting transfers between devices, local(): far = lax.ppermute(far, RING, ring_perm(1))  13.9 us
    all_to_all x1, blocking collectives, local(): held = lax.all_to_all(held, 'dp', 0, 0, axis_index_groups=X_GROUPS)  11.9 us
    ppermute x1, starting transfers between devices, local(): sibling = lax.ppermute(weight_down, 'wout', CORE_SWAP)  11.3 us
    ppermute x2, starting transfers between devices, local(): lax.ppermute(windows[j], 'dp', zh_perm(j))  10.6 us
    pallas_call x2, Pallas kernels, product(): pl.pallas_call(functools.partial(product_kernel, len(blocks)), in_specs=[...  6.32 us
    ppermute x2, starting transfers between devices, local(): behind = lax.ppermute(behind, RING, ring_perm(-1))  6.1 us
  transfers between devices with their start and end apart: 13, of which 7 were waited for; matrix products, arithmetic and copies ran while one was open for 0% of the time, Pallas kernels for 5%

profile of v2, /device:TPU:1, one launch (start us, length us, event | category | flops | bytes accessed | tf_op | source)
XLA Modules:
  0.0 134.4 jit_solution(16703498905544113947)
XLA Ops:
  0.0 0.0 copy-start
  0.0 0.0 copy-start.2
  0.0 1.2 copy-done.2
  1.2 0.0 copy-start.3
  1.2 0.9 copy-done.3
  2.2 0.6 shard_map.46
  2.8 11.9 %all_to_all.5.in_ref = bf16[4,48,1536]{2,1,0:T(8,128)(2,1)S(1)} all-to-all(bf16[4,48,1536]{2,1,0:T(8,128)(2,1)S(1)} %shard_map.46), channel_id=1, replica_groups={{0,192,384,576},{64,256,448,640},{128,320,512,704},{1,193,385,577},{65,..., dimensions={0} | all-to-all | bytes 1179648 | tf_op jit(solution)/shard_map/all_to_all | solution.py:188
  14.7 0.8 shard_map.47
  15.5 11.3 %collective-permute-start.2 = (bf16[1536,1536]{1,0:T(8,128)(2,1)}, bf16[1536,1536]{1,0:T(8,128)(2,1)S(1)}, u32[]{:S(2)}, u32[]{:S(2)}) collective-permute-start(bf16[1536,1536]{1,0:T(8,128)(2,1)} %refs_3_), channel_id=1, source_target_pairs={{0,4},{4,0},{8,12},{12,8},{16,20},{20,16},{24,28},{28,24},{32,36},... | collective-permute-start | bytes 14155784 | tf_op jit(solution)/shard_map/ppermute | solution.py:191
  26.9 5.1 %collective-permute-start = (bf16[64,1536]{1,0:T(8,128)(2,1)S(1)}, bf16[64,1536]{1,0:T(8,128)(2,1)S(1)}, u32[]{:S(2)}, u32[]{:S(2)}) collective-permute-start(bf16[64,1536]{1,0:T(8,128)(2,1)S(1)} %get-tuple-element.23), channel_id=1, source_target_pairs={{0,64},{64,128},{128,0},{192,256},{256,320},{320,192},{384,448},{4... | collective-permute-start | bytes 589832 | tf_op jit(solution)/shard_map/ppermute | solution.py:201
  32.0 5.6 %collective-permute-start.1 = (bf16[64,1536]{1,0:T(8,128)(2,1)S(1)}, bf16[64,1536]{1,0:T(8,128)(2,1)S(1)}, u32[]{:S(2)}, u32[]{:S(2)}) collective-permute-start(bf16[64,1536]{1,0:T(8,128)(2,1)S(1)} %get-tuple-element.24), channel_id=1, source_target_pairs={{0,128},{64,0},{128,64},{192,320},{256,192},{320,256},{384,512},{4... | collective-permute-start | bytes 589832 | tf_op jit(solution)/shard_map/ppermute | solution.py:201
  37.5 3.4 %collective-permute-done.refs_1_ = bf16[64,1536]{1,0:T(8,128)(2,1)S(1)} collective-permute-done((bf16[64,1536]{1,0:T(8,128)(2,1)S(1)}, bf16[64,1536]{1,0:T(8,128)(2,1)S(1)}, u32[]{:S(2)}, u32[]{:S(2)}) %collective-permute-start) | collective-permute-done | bytes 196640 | tf_op jit(solution)/shard_map/ppermute | solution.py:201
  41.0 14.7 %collective-permute-done.1.refs_2_ = bf16[64,1536]{1,0:T(8,128)(2,1)S(1)} collective-permute-done((bf16[64,1536]{1,0:T(8,128)(2,1)S(1)}, bf16[64,1536]{1,0:T(8,128)(2,1)S(1)}, u32[]{:S(2)}, u32[]{:S(2)}) %collective-permute-start.1) | collective-permute-done | bytes 196640 | tf_op jit(solution)/shard_map/ppermute | solution.py:201
  55.7 0.7 shard_map.48
  56.4 18.3 %all-gather = bf16[256,1536]{1,0:T(8,128)(2,1)S(1)} all-gather(bf16[64,1536]{1,0:T(8,128)(2,1)S(1)} %shard_map.48), channel_id=2, replica_groups={{0,16,32,48},{4,20,36,52},{8,24,40,56},{12,28,44,60},{1,17,33,49},{5,21..., dimensions={0}, use_global_device_ids=true | all-gather | bytes 983040 | tf_op jit(solution)/shard_map/all_gather | solution.py:203
  74.7 0.1 fusion
  74.7 2.2 %collective-permute-start.6 = (bf16[2,64,1536]{2,1,0:T(8,128)(2,1)S(1)}, bf16[2,64,1536]{2,1,0:T(8,128)(2,1)S(1)}, u32[]{:S(2)}, u32[]{:S(2)}) collective-permute-start(bf16[2,64,1536]{2,1,0:T(8,128)(2,1)S(1)} %bitcast.8), channel_id=1, source_target_pairs={{0,8},{4,12},{8,16},{12,20},{16,24},{20,28},{24,32},{28,36},{32,40... | collective-permute-start | bytes 1179656 | tf_op jit(solution)/shard_map/ppermute | solution.py:205
  76.9 4.3 %collective-permute-start.7 = (bf16[2,64,1536]{2,1,0:T(8,128)(2,1)S(1)}, bf16[2,64,1536]{2,1,0:T(8,128)(2,1)S(1)}, u32[]{:S(2)}, u32[]{:S(2)}) collective-permute-start(bf16[2,64,1536]{2,1,0:T(8,128)(2,1)S(1)} %bitcast.7), channel_id=1, source_target_pairs={{0,56},{4,60},{8,0},{12,4},{16,8},{20,12},{24,16},{28,20},{32,24},... | collective-permute-start | bytes 1179656 | tf_op jit(solution)/shard_map/ppermute | solution.py:206
  81.3 0.0 collective-permute-done.2.refs_1_.refs_2_
  81.3 0.0 copy-done
  81.3 0.0 copy-start.1
  81.3 3.2 %shard_map.49 = (bf16[64,3072]{1,0:T(8,128)(2,1)S(1)}, bf16[64,3072]{1,0:T(8,128)(2,1)S(1)}, bf16[64,3072]{1,0:T(8,128)(2,1)S(1)}, bf16[64,3072]{1,0:T(8,128)(2,1)S(1)}) custom-call(bf16[4,64,1536]{2,1,0:T(8,128)(2,1)S(1)} %bitcast.5, bf16[1536,1536]{1,0:T(8,128)(2,1)S(1)} %collective-permute-done.2.refs_1_.refs_2_, bf16[1536,1536]{1,0:T(8,128)(2,1)S(1)} %copy-done), custom_call_target="tpu_custom_call" | custom-call | tf_op jit(solution)/shard_map/pallas_call | solution.py:128
  84.5 7.2 %collective-permute-start.3 = (bf16[64,3072]{1,0:T(8,128)(2,1)S(1)}, bf16[64,3072]{1,0:T(8,128)(2,1)S(1)}, u32[]{:S(2)}, u32[]{:S(2)}) collective-permute-start(bf16[64,3072]{1,0:T(8,128)(2,1)S(1)} %get-tuple-element.28), channel_id=1, source_target_pairs={{0,1},{4,135},{8,9},{12,143},{16,17},{20,151},{24,25},{28,159},{32... | collective-permute-start | bytes 1179656 | tf_op jit(solution)/shard_map/ppermute | solution.py:212
  91.7 0.0 copy-done.1
  91.7 0.1 shard_map.51
  91.8 2.0 %collective-permute-start.11 = (bf16[2,4,16,1536]{3,2,1,0:T(8,128)(2,1)S(1)}, bf16[2,4,16,1536]{3,2,1,0:T(8,128)(2,1)S(1)}, u32[]{:S(2)}, u32[]{:S(2)}) collective-permute-start(bf16[2,4,16,1536]{3,2,1,0:T(8,128)(2,1)S(1)} %get-tuple-element.36), channel_id=1, source_target_pairs={{0,4},{4,0},{8,12},{12,8},{16,20},{20,16},{24,28},{28,24},{32,36},... | collective-permute-start | bytes 1179656 | tf_op jit(solution)/shard_map/ppermute | solution.py:200
  93.7 2.4 %collective-permute-start.5 = (bf16[64,3072]{1,0:T(8,128)(2,1)S(1)}, bf16[64,3072]{1,0:T(8,128)(2,1)S(1)}, u32[]{:S(2)}, u32[]{:S(2)}) collective-permute-start(bf16[64,3072]{1,0:T(8,128)(2,1)S(1)} %get-tuple-element.29), channel_id=1, source_target_pairs={{0,131},{4,5},{8,139},{12,13},{16,147},{20,21},{24,155},{28,29},{3... | collective-permute-start | bytes 1179656 | tf_op jit(solution)/shard_map/ppermute | solution.py:213
  96.1 0.0 collective-permute-done.6.refs_0_
  96.1 0.0 collective-permute-done.7.refs_1_
  96.1 3.2 %shard_map.50 = (bf16[64,3072]{1,0:T(8,128)(2,1)S(1)}, bf16[64,3072]{1,0:T(8,128)(2,1)S(1)}, bf16[64,3072]{1,0:T(8,128)(2,1)S(1)}, bf16[64,3072]{1,0:T(8,128)(2,1)S(1)}) custom-call(bf16[2,64,1536]{2,1,0:T(8,128)(2,1)S(1)} %collective-permute-done.6.refs_0_, bf16[2,64,1536]{2,1,0:T(8,128)(2,1)S(1)} %collective-permute-done.7.refs_1_, ...), custom_call_target="tpu_custom_call" | custom-call | tf_op jit(solution)/shard_map/pallas_call | solution.py:128
  99.3 6.7 %collective-permute-start.8 = (bf16[64,3072]{1,0:T(8,128)(2,1)S(1)}, bf16[64,3072]{1,0:T(8,128)(2,1)S(1)}, u32[]{:S(2)}, u32[]{:S(2)}) collective-permute-start(bf16[64,3072]{1,0:T(8,128)(2,1)S(1)} %get-tuple-element.32), channel_id=1, source_target_pairs={{0,1},{4,135},{8,9},{12,143},{16,17},{20,151},{24,25},{28,159},{32... | collective-permute-start | bytes 1179656 | tf_op jit(solution)/shard_map/ppermute | solution.py:212
  106.0 3.7 %collective-permute-start.10 = (bf16[64,3072]{1,0:T(8,128)(2,1)S(1)}, bf16[64,3072]{1,0:T(8,128)(2,1)S(1)}, u32[]{:S(2)}, u32[]{:S(2)}) collective-permute-start(bf16[64,3072]{1,0:T(8,128)(2,1)S(1)} %get-tuple-element.33), channel_id=1, source_target_pairs={{0,131},{4,5},{8,139},{12,13},{16,147},{20,21},{24,155},{28,29},{3... | collective-permute-start | bytes 1179656 | tf_op jit(solution)/shard_map/ppermute | solution.py:213
  109.8 0.0 collective-permute-done.3
  109.8 0.1 add_convert_fusion.1
  109.9 2.8 %collective-permute-start.4 = (bf16[64,3072]{1,0:T(8,128)(2,1)S(1)}, bf16[64,3072]{1,0:T(8,128)(2,1)S(1)}, u32[]{:S(2)}, u32[]{:S(2)}) collective-permute-start(bf16[64,3072]{1,0:T(8,128)(2,1)S(1)} %add_convert_fusion.1), channel_id=1, source_target_pairs={{0,1},{4,135},{8,9},{12,143},{16,17},{20,151},{24,25},{28,159},{32... | collective-permute-start | bytes 1179656 | tf_op jit(solution)/shard_map/ppermute | solution.py:215
  112.6 2.4 %collective-permute-done.8 = bf16[64,3072]{1,0:T(8,128)(2,1)S(1)} collective-permute-done((bf16[64,3072]{1,0:T(8,128)(2,1)S(1)}, bf16[64,3072]{1,0:T(8,128)(2,1)S(1)}, u32[]{:S(2)}, u32[]{:S(2)}) %collective-permute-start.8) | collective-permute-done | bytes 393248 | tf_op jit(solution)/shard_map/ppermute | solution.py:212
  115.0 0.1 add_convert_fusion
  115.1 1.9 %collective-permute-start.9 = (bf16[64,3072]{1,0:T(8,128)(2,1)S(1)}, bf16[64,3072]{1,0:T(8,128)(2,1)S(1)}, u32[]{:S(2)}, u32[]{:S(2)}) collective-permute-start(bf16[64,3072]{1,0:T(8,128)(2,1)S(1)} %add_convert_fusion), channel_id=1, source_target_pairs={{0,1},{4,135},{8,9},{12,143},{16,17},{20,151},{24,25},{28,159},{32... | collective-permute-start | bytes 1179656 | tf_op jit(solution)/shard_map/ppermute | solution.py:215
  117.0 0.0 collective-permute-done.11.refs_7_
  117.1 0.0 collective-permute-done.5.refs_2_
  117.1 3.2 %collective-permute-done.10.refs_5_ = bf16[64,3072]{1,0:T(8,128)(2,1)S(1)} collective-permute-done((bf16[64,3072]{1,0:T(8,128)(2,1)S(1)}, bf16[64,3072]{1,0:T(8,128)(2,1)S(1)}, u32[]{:S(2)}, u32[]{:S(2)}) %collective-permute-start.10) | collective-permute-done | bytes 393248 | tf_op jit(solution)/shard_map/ppermute | solution.py:213
  120.3 1.4 %collective-permute-done.4.refs_1_ = bf16[64,3072]{1,0:T(8,128)(2,1)S(1)} collective-permute-done((bf16[64,3072]{1,0:T(8,128)(2,1)S(1)}, bf16[64,3072]{1,0:T(8,128)(2,1)S(1)}, u32[]{:S(2)}, u32[]{:S(2)}) %collective-permute-start.4) | collective-permute-done | bytes 393248 | tf_op jit(solution)/shard_map/ppermute | solution.py:215
  121.7 4.2 %collective-permute-done.9.refs_4_ = bf16[64,3072]{1,0:T(8,128)(2,1)S(1)} collective-permute-done((bf16[64,3072]{1,0:T(8,128)(2,1)S(1)}, bf16[64,3072]{1,0:T(8,128)(2,1)S(1)}, u32[]{:S(2)}, u32[]{:S(2)}) %collective-permute-start.9) | collective-permute-done | bytes 393248 | tf_op jit(solution)/shard_map/ppermute | solution.py:215
  125.9 0.9 shard_map.52
  126.9 5.3 %collective-permute-start.12 = (bf16[2,4,16,1536]{3,2,1,0:T(8,128)(2,1)S(1)}, bf16[2,4,16,1536]{3,2,1,0:T(8,128)(2,1)S(1)}, u32[]{:S(2)}, u32[]{:S(2)}) collective-permute-start(bf16[2,4,16,1536]{3,2,1,0:T(8,128)(2,1)S(1)} %get-tuple-element.38), channel_id=1, source_target_pairs={{0,4},{4,0},{8,12},{12,8},{16,20},{20,16},{24,28},{28,24},{32,36},... | collective-permute-start | bytes 1179656 | tf_op jit(solution)/shard_map/ppermute | solution.py:224
  132.1 1.3 collective-permute-done.12.other_ref
  133.5 1.0 shard_map.53
Async XLA Ops:
  0.0 81.3 %copy-start = (bf16[1536,1536]{1,0:T(8,128)(2,1)S(1)}, bf16[1536,1536]{1,0:T(8,128)(2,1)}, u32[]{:S(2)}) copy-start(bf16[1536,1536]{1,0:T(8,128)(2,1)} %refs_3_) | copy-start | bytes 14155780
  0.0 1.2 copy-start.2
  1.2 0.9 copy-start.3
  15.5 65.7 %collective-permute-start.2 = (bf16[1536,1536]{1,0:T(8,128)(2,1)}, bf16[1536,1536]{1,0:T(8,128)(2,1)S(1)}, u32[]{:S(2)}, u32[]{:S(2)}) collective-permute-start(bf16[1536,1536]{1,0:T(8,128)(2,1)} %refs_3_), channel_id=1, source_target_pairs={{0,4},{4,0},{8,12},{12,8},{16,20},{20,16},{24,28},{28,24},{32,36},... | collective-permute-start | bytes 14155784 | tf_op jit(solution)/shard_map/ppermute | solution.py:191
  26.9 14.1 %collective-permute-start = (bf16[64,1536]{1,0:T(8,128)(2,1)S(1)}, bf16[64,1536]{1,0:T(8,128)(2,1)S(1)}, u32[]{:S(2)}, u32[]{:S(2)}) collective-permute-start(bf16[64,1536]{1,0:T(8,128)(2,1)S(1)} %get-tuple-element.23), channel_id=1, source_target_pairs={{0,64},{64,128},{128,0},{192,256},{256,320},{320,192},{384,448},{4... | collective-permute-start | bytes 589832 | tf_op jit(solution)/shard_map/ppermute | solution.py:201
  32.0 23.7 %collective-permute-start.1 = (bf16[64,1536]{1,0:T(8,128)(2,1)S(1)}, bf16[64,1536]{1,0:T(8,128)(2,1)S(1)}, u32[]{:S(2)}, u32[]{:S(2)}) collective-permute-start(bf16[64,1536]{1,0:T(8,128)(2,1)S(1)} %get-tuple-element.24), channel_id=1, source_target_pairs={{0,128},{64,0},{128,64},{192,320},{256,192},{320,256},{384,512},{4... | collective-permute-start | bytes 589832 | tf_op jit(solution)/shard_map/ppermute | solution.py:201
  74.7 21.4 %collective-permute-start.6 = (bf16[2,64,1536]{2,1,0:T(8,128)(2,1)S(1)}, bf16[2,64,1536]{2,1,0:T(8,128)(2,1)S(1)}, u32[]{:S(2)}, u32[]{:S(2)}) collective-permute-start(bf16[2,64,1536]{2,1,0:T(8,128)(2,1)S(1)} %bitcast.8), channel_id=1, source_target_pairs={{0,8},{4,12},{8,16},{12,20},{16,24},{20,28},{24,32},{28,36},{32,40... | collective-permute-start | bytes 1179656 | tf_op jit(solution)/shard_map/ppermute | solution.py:205
  76.9 19.2 %collective-permute-start.7 = (bf16[2,64,1536]{2,1,0:T(8,128)(2,1)S(1)}, bf16[2,64,1536]{2,1,0:T(8,128)(2,1)S(1)}, u32[]{:S(2)}, u32[]{:S(2)}) collective-permute-start(bf16[2,64,1536]{2,1,0:T(8,128)(2,1)S(1)} %bitcast.7), channel_id=1, source_target_pairs={{0,56},{4,60},{8,0},{12,4},{16,8},{20,12},{24,16},{28,20},{32,24},... | collective-permute-start | bytes 1179656 | tf_op jit(solution)/shard_map/ppermute | solution.py:206
  81.3 10.4 %copy-start.1 = (bf16[256,1536]{1,0:T(8,128)(2,1)S(1)}, bf16[256,1536]{1,0:T(8,128)(2,1)}, u32[]{:S(2)}) copy-start(bf16[256,1536]{1,0:T(8,128)(2,1)} %param.7) | copy-start | bytes 2359300
  84.5 25.3 %collective-permute-start.3 = (bf16[64,3072]{1,0:T(8,128)(2,1)S(1)}, bf16[64,3072]{1,0:T(8,128)(2,1)S(1)}, u32[]{:S(2)}, u32[]{:S(2)}) collective-permute-start(bf16[64,3072]{1,0:T(8,128)(2,1)S(1)} %get-tuple-element.28), channel_id=1, source_target_pairs={{0,1},{4,135},{8,9},{12,143},{16,17},{20,151},{24,25},{28,159},{32... | collective-permute-start | bytes 1179656 | tf_op jit(solution)/shard_map/ppermute | solution.py:212
  91.8 25.3 %collective-permute-start.11 = (bf16[2,4,16,1536]{3,2,1,0:T(8,128)(2,1)S(1)}, bf16[2,4,16,1536]{3,2,1,0:T(8,128)(2,1)S(1)}, u32[]{:S(2)}, u32[]{:S(2)}) collective-permute-start(bf16[2,4,16,1536]{3,2,1,0:T(8,128)(2,1)S(1)} %get-tuple-element.36), channel_id=1, source_target_pairs={{0,4},{4,0},{8,12},{12,8},{16,20},{20,16},{24,28},{28,24},{32,36},... | collective-permute-start | bytes 1179656 | tf_op jit(solution)/shard_map/ppermute | solution.py:200
  93.7 23.3 %collective-permute-start.5 = (bf16[64,3072]{1,0:T(8,128)(2,1)S(1)}, bf16[64,3072]{1,0:T(8,128)(2,1)S(1)}, u32[]{:S(2)}, u32[]{:S(2)}) collective-permute-start(bf16[64,3072]{1,0:T(8,128)(2,1)S(1)} %get-tuple-element.29), channel_id=1, source_target_pairs={{0,131},{4,5},{8,139},{12,13},{16,147},{20,21},{24,155},{28,29},{3... | collective-permute-start | bytes 1179656 | tf_op jit(solution)/shard_map/ppermute | solution.py:213
  99.3 15.7 %collective-permute-start.8 = (bf16[64,3072]{1,0:T(8,128)(2,1)S(1)}, bf16[64,3072]{1,0:T(8,128)(2,1)S(1)}, u32[]{:S(2)}, u32[]{:S(2)}) collective-permute-start(bf16[64,3072]{1,0:T(8,128)(2,1)S(1)} %get-tuple-element.32), channel_id=1, source_target_pairs={{0,1},{4,135},{8,9},{12,143},{16,17},{20,151},{24,25},{28,159},{32... | collective-permute-start | bytes 1179656 | tf_op jit(solution)/shard_map/ppermute | solution.py:212
  106.0 14.3 %collective-permute-start.10 = (bf16[64,3072]{1,0:T(8,128)(2,1)S(1)}, bf16[64,3072]{1,0:T(8,128)(2,1)S(1)}, u32[]{:S(2)}, u32[]{:S(2)}) collective-permute-start(bf16[64,3072]{1,0:T(8,128)(2,1)S(1)} %get-tuple-element.33), channel_id=1, source_target_pairs={{0,131},{4,5},{8,139},{12,13},{16,147},{20,21},{24,155},{28,29},{3... | collective-permute-start | bytes 1179656 | tf_op jit(solution)/shard_map/ppermute | solution.py:213
  109.9 11.8 %collective-permute-start.4 = (bf16[64,3072]{1,0:T(8,128)(2,1)S(1)}, bf16[64,3072]{1,0:T(8,128)(2,1)S(1)}, u32[]{:S(2)}, u32[]{:S(2)}) collective-permute-start(bf16[64,3072]{1,0:T(8,128)(2,1)S(1)} %add_convert_fusion.1), channel_id=1, source_target_pairs={{0,1},{4,135},{8,9},{12,143},{16,17},{20,151},{24,25},{28,159},{32... | collective-permute-start | bytes 1179656 | tf_op jit(solution)/shard_map/ppermute | solution.py:215
  115.1 10.8 %collective-permute-start.9 = (bf16[64,3072]{1,0:T(8,128)(2,1)S(1)}, bf16[64,3072]{1,0:T(8,128)(2,1)S(1)}, u32[]{:S(2)}, u32[]{:S(2)}) collective-permute-start(bf16[64,3072]{1,0:T(8,128)(2,1)S(1)} %add_convert_fusion), channel_id=1, source_target_pairs={{0,1},{4,135},{8,9},{12,143},{16,17},{20,151},{24,25},{28,159},{32... | collective-permute-start | bytes 1179656 | tf_op jit(solution)/shard_map/ppermute | solution.py:215
  126.9 6.6 %collective-permute-start.12 = (bf16[2,4,16,1536]{3,2,1,0:T(8,128)(2,1)S(1)}, bf16[2,4,16,1536]{3,2,1,0:T(8,128)(2,1)S(1)}, u32[]{:S(2)}, u32[]{:S(2)}) collective-permute-start(bf16[2,4,16,1536]{3,2,1,0:T(8,128)(2,1)S(1)} %get-tuple-element.38), channel_id=1, source_target_pairs={{0,4},{4,0},{8,12},{12,8},{16,20},{20,16},{24,28},{28,24},{32,36},... | collective-permute-start | bytes 1179656 | tf_op jit(solution)/shard_map/ppermute | solution.py:224

commit v3 on v2

--- a/solution.py
+++ b/solution.py
@@ -1,5 +1,3 @@
-import functools
-
 import jax
 import jax.numpy as jnp
 from jax import lax
@@ -19,6 +17,7 @@
 X_GROUPS = [[x * NZH + z for x in range(NX)] for z in range(NZH)]
 PARITY_GROUPS = [[y * 2 + c for y in range(p, NY, 2)] for p in range(2) for c in range(2)]
 CORE_SWAP = [(w, w ^ 1) for w in range(2 * NY)]
+PAIR_SWAP = [(w, w ^ 2) for w in range(2 * NY)]
 RING = ("dp", "wout", "win")
 
 
@@ -40,10 +39,6 @@
 
 def zh_perm(step):
     return [(x * NZH + z, x * NZH + (z + step) % NZH) for x in range(NX) for z in range(NZH)]
-
-
-def y_perm(step):
-    return [(y * 2 + c, (y + step) % NY * 2 + c) for y in range(NY) for c in range(2)]
 
 
 def params():
@@ -93,18 +88,13 @@
         out_ref[rows] = block
 
 
-def product_kernel(count, *refs):
-    rows_refs, (sibling_ref, own_hbm), out_refs = refs[:count], refs[count:count + 2], refs[count + 2:-2]
-    own_ref, sem = refs[-2:]
+def product_kernel(rows_ref, sibling_ref, own_hbm, *refs):
+    out_refs, (own_ref, sem) = refs[:-2], refs[-2:]
     copy = pltpu.make_async_copy(own_hbm, own_ref, sem)
     copy.start()
     hidden, width = sibling_ref.shape
     rows = jnp.concatenate(
-        [
-            ref[:, s * ROWS:(s + 1) * ROWS].reshape(-1, width)
-            for s in range(SLOTS) for ref in rows_refs
-        ],
-        axis=0,
+        [rows_ref[:, s * ROWS:(s + 1) * ROWS].reshape(-1, width) for s in range(SLOTS)], axis=0
     )
 
     def run(weight_ref, start):
@@ -126,13 +116,13 @@
     hidden, width = own.shape
     vmem = pl.BlockSpec(memory_space=pltpu.VMEM)
     return pl.pallas_call(
-        functools.partial(product_kernel, len(blocks)),
-        in_specs=[vmem] * (len(blocks) + 1) + [pl.BlockSpec(memory_space=pl.ANY)],
+        product_kernel,
+        in_specs=[vmem] * 2 + [pl.BlockSpec(memory_space=pl.ANY)],
         out_specs=[vmem] * SLOTS,
         out_shape=[jax.ShapeDtypeStruct((HALF * ROWS, 2 * hidden), jnp.bfloat16)] * SLOTS,
         scratch_shapes=[pltpu.VMEM((hidden, width), jnp.bfloat16), pltpu.SemaphoreType.DMA],
         compiler_params=params(),
-    )(*blocks, sibling, own)
+    )(blocks, sibling, own)
 
 
 def parity_and_core():
@@ -140,32 +130,37 @@
     return place // 2 % 2, place % 2
 
 
-def split_kernel(pre_ref, kept_ref, sent_ref):
+def half_sums(parts, j, i, hidden):
+    total = 0.0
+    for ref in parts:
+        total = total + ref[j * ROWS:(j + 1) * ROWS, i * hidden:(i + 1) * hidden].astype(jnp.float32)
+    return total
+
+
+def send_kernel(*refs):
+    parts, sent_ref = (refs[:3], refs[3:6]), refs[6]
+    for h in range(2):
+        for j in range(HALF):
+            sent_ref[h, j] = half_sums(parts[h], j, 1, sent_ref.shape[3]).astype(jnp.bfloat16)
+
+
+def keep_kernel(*refs):
+    parts, (pre_ref, kept_ref, slope_ref) = (refs[:3], refs[3:6]), refs[6:]
     parity, core = parity_and_core()
     for h in range(2):
         for j in range(HALF):
-            kept_ref[h, j] = pre_ref[j, (parity + h) % 2, core]
-            sent_ref[h, j] = pre_ref[j, (parity + h) % 2, 1 - core]
-
-
-def finish_kernel(*refs):
-    parts, (pre_own, pre_sibling, kept_ref, sent_ref) = refs[:6], refs[6:]
-    hidden = pre_own.shape[3]
-    for h in range(2):
-        mine, ahead, behind = parts[3 * h:3 * h + 3]
-        for i, (pre_ref, out_ref) in enumerate(((pre_own, kept_ref), (pre_sibling, sent_ref))):
-            for j in range(HALF):
-                at = slice(j * ROWS, (j + 1) * ROWS), slice(i * hidden, (i + 1) * hidden)
-                total = mine[at].astype(jnp.float32) + ahead[at].astype(jnp.float32) + behind[at].astype(jnp.float32)
-                out_ref[h, j] = (total * gelu_slope(pre_ref[h, j].astype(jnp.float32))).astype(jnp.bfloat16)
-
-
-def join_kernel(kept_ref, other_ref, out_ref):
+            slope = gelu_slope(pre_ref[j, (parity + h) % 2, core].astype(jnp.float32))
+            kept_ref[h, j] = (half_sums(parts[h], j, 0, kept_ref.shape[3]) * slope).astype(jnp.bfloat16)
+            slope_ref[h, j] = gelu_slope(pre_ref[j, (parity + h) % 2, 1 - core].astype(jnp.float32))
+
+
+def join_kernel(kept_ref, slope_ref, other_ref, out_ref):
     parity, core = parity_and_core()
     for h in range(2):
         for j in range(HALF):
             out_ref[j, (parity + h) % 2, core] = kept_ref[h, j]
-            out_ref[j, (parity + h) % 2, 1 - core] = other_ref[h, j]
+            other = other_ref[h, j].astype(jnp.float32) * slope_ref[h, j]
+            out_ref[j, (parity + h) % 2, 1 - core] = other.astype(jnp.bfloat16)
 
 
 def local(returned, lang_rank, weight_down, pre_act):
@@ -187,48 +182,40 @@
     held = move(rank_blocks_kernel, (NX, NZH * ROWS), returned)
     held = lax.all_to_all(held, "dp", 0, 0, axis_index_groups=X_GROUPS)
     windows = move(window_blocks_kernel, (SLOTS * ROWS,), held, count=NZH)
-    weight_down, pre_act, _ = lax.optimization_barrier((weight_down, pre_act, windows[1]))
-    sibling = lax.ppermute(weight_down, "wout", CORE_SWAP)
-    halves = jax.ShapeDtypeStruct((2, HALF, ROWS, hidden), jnp.bfloat16)
-    pre_own, pre_sent = pl.pallas_call(
-        split_kernel,
-        in_specs=[vmem],
-        out_specs=[vmem] * 2,
-        out_shape=[halves] * 2,
-        compiler_params=params(),
-    )(pre_act.reshape(HALF, 2, 2, ROWS, hidden))
-    pre_sibling = lax.ppermute(pre_sent, "wout", CORE_SWAP)
+    weight_sent, _ = lax.optimization_barrier((weight_down, windows[1]))
+    sibling = lax.ppermute(weight_sent, "wout", CORE_SWAP)
     windows = [windows[0]] + [lax.ppermute(windows[j], "dp", zh_perm(j)) for j in range(1, NZH)]
     window = move(window_pick_kernel, (SLOTS * ROWS,), *windows)
     near = lax.all_gather(window, "wout", axis_index_groups=PARITY_GROUPS)
-    others = [
-        lax.ppermute(near[:HALF // 2], "wout", y_perm(1)),
-        lax.ppermute(near[HALF // 2:], "wout", y_perm(-1)),
-    ]
+    others = lax.ppermute(near, "wout", PAIR_SWAP)
 
     parts = []
-    for blocks in ([near], others):
+    for blocks in (near, others):
         far, ahead, behind, mine = product(blocks, weight_down, sibling)
         far = lax.ppermute(far, RING, ring_perm(1))
         behind = lax.ppermute(behind, RING, ring_perm(-1))
         ahead = (ahead.astype(jnp.float32) + far.astype(jnp.float32)).astype(jnp.bfloat16)
         parts += [mine, lax.ppermute(ahead, RING, ring_perm(1)), behind]
 
-    kept, sent = pl.pallas_call(
-        finish_kernel,
-        in_specs=[vmem] * 8,
-        out_specs=[vmem] * 2,
-        out_shape=[halves] * 2,
-        compiler_params=params(),
-    )(*parts, pre_own, pre_sibling)
+    def call(kernel, shapes, *values):
+        return pl.pallas_call(
+            kernel,
+            in_specs=[vmem] * len(values),
+            out_specs=[vmem] * len(shapes),
+            out_shape=[jax.ShapeDtypeStruct(*shape) for shape in shapes],
+            compiler_params=params(),
+        )(*values)
+
+    halves = (2, HALF, ROWS, hidden)
+    split = (HALF, 2, 2, ROWS, hidden)
+    (sent,) = call(send_kernel, [(halves, jnp.bfloat16)], *parts)
     other = lax.ppermute(sent, "wout", CORE_SWAP)
-    out = pl.pallas_call(
-        join_kernel,
-        in_specs=[vmem] * 2,
-        out_specs=vmem,
-        out_shape=jax.ShapeDtypeStruct((HALF, 2, 2, ROWS, hidden), jnp.bfloat16),
-        compiler_params=params(),
-    )(kept, other)
+    kept, slope = call(
+        keep_kernel,
+        [(halves, jnp.bfloat16), (halves, jnp.float32)],
+        *parts, pre_act.reshape(split),
+    )
+    (out,) = call(join_kernel, [(split, jnp.bfloat16)], kept, slope, other)
     return out.reshape(2 * NY * ROWS, hidden)
 
 

time: 135 us -> 131 us (0.970)
  starting transfers between devices: 60.4 us -> 57.2 us
    ppermute x4 -> x2, starting transfers between devices: 19.8 us -> 13.5 us  [the longest x1 11.3 us: local(): sibling = lax.ppermute(weight_sent, 'wout', CORE_SWAP)]
    ppermute x2, starting transfers between devices: 4.68 us -> 7.66 us  [local(): parts += [mine, lax.ppermute(ahead, RING, ring_perm(1)), behind]]
    ppermute x1, starting transfers between devices: 5.26 us -> 7.77 us  [local(): other = lax.ppermute(sent, 'wout', CORE_SWAP)]
    ppermute x2, waiting for transfers between devices: 2.38 us -> 0.01 us  [local(): far = lax.ppermute(far, RING, ring_perm(1))]
    ppermute x2, starting transfers between devices: 6.1 us -> 3.84 us  [local(): behind = lax.ppermute(behind, RING, ring_perm(-1))]
    ppermute x4 -> x2, waiting for transfers between devices: 0.01 us -> 1.64 us  [the longest x1 1.63 us: local(): others = lax.ppermute(near, 'wout', PAIR_SWAP)]
    ppermute x2, waiting for transfers between devices: 5.64 us -> 7.22 us  [local(): parts += [mine, lax.ppermute(ahead, RING, ring_perm(1)), behind]]
  transfers between devices with their start and end apart: 13 -> 11, of which waited for: 7 -> 7; matrix products, arithmetic and copies ran while one was open for 0% -> 0% of each run, Pallas kernels for 5% -> 6%
where the time goes in v3:
time: 131 us
  starting transfers between devices  57.2 us (44%)
  blocking collectives  30.2 us (23%)
  waiting for transfers between devices  30.2 us (23%)
  Pallas kernels  10.3 us (8%)
  local copies, waits for them, and re-layouts  2.17 us (2%)
    all_gather x1, blocking collectives, local(): near = lax.all_gather(window, 'wout', axis_index_groups=PARITY_GROUPS)  18.3 us
    ppermute x2, waiting for transfers between devices, local(): lax.ppermute(windows[j], 'dp', zh_perm(j))  18.2 us
    ppermute x2, starting transfers between devices, local(): far = lax.ppermute(far, RING, ring_perm(1))  13.8 us
    all_to_all x1, blocking collectives, local(): held = lax.all_to_all(held, 'dp', 0, 0, axis_index_groups=X_GROUPS)  11.9 us
    ppermute x1, starting transfers between devices, local(): sibling = lax.ppermute(weight_sent, 'wout', CORE_SWAP)  11.3 us
    ppermute x2, starting transfers between devices, local(): lax.ppermute(windows[j], 'dp', zh_perm(j))  10.6 us
    ppermute x1, starting transfers between devices, local(): other = lax.ppermute(sent, 'wout', CORE_SWAP)  7.77 us
    ppermute x2, starting transfers between devices, local(): parts += [mine, lax.ppermute(ahead, RING, ring_perm(1)), behind]  7.66 us
  transfers between devices with their start and end apart: 11, of which 7 were waited for; matrix products, arithmetic and copies ran while one was open for 0% of the time, Pallas kernels for 6%

profile of v3, /device:TPU:1, one launch (start us, length us, event | category | flops | bytes accessed | tf_op | source)
XLA Modules:
  0.0 130.6 jit_solution(13993166320165057437)
XLA Ops:
  0.0 0.0 copy-start
  0.0 0.0 copy-start.2
  0.0 1.2 copy-done.2
  1.2 0.0 copy-start.3
  1.2 0.9 copy-done.3
  2.2 0.6 shard_map.46
  2.8 11.9 %all_to_all.5.in_ref = bf16[4,48,1536]{2,1,0:T(8,128)(2,1)S(1)} all-to-all(bf16[4,48,1536]{2,1,0:T(8,128)(2,1)S(1)} %shard_map.46), channel_id=1, replica_groups={{0,192,384,576},{64,256,448,640},{128,320,512,704},{1,193,385,577},{65,..., dimensions={0} | all-to-all | bytes 1179648 | tf_op jit(solution)/shard_map/all_to_all | solution.py:183
  14.7 0.8 shard_map.47
  15.5 11.3 %collective-permute-start.2 = (bf16[1536,1536]{1,0:T(8,128)(2,1)}, bf16[1536,1536]{1,0:T(8,128)(2,1)S(1)}, u32[]{:S(2)}, u32[]{:S(2)}) collective-permute-start(bf16[1536,1536]{1,0:T(8,128)(2,1)} %own_hbm.3), channel_id=1, source_target_pairs={{0,4},{4,0},{8,12},{12,8},{16,20},{20,16},{24,28},{28,24},{32,36},... | collective-permute-start | bytes 14155784 | tf_op jit(solution)/shard_map/ppermute | solution.py:186
  26.9 5.1 %collective-permute-start = (bf16[64,1536]{1,0:T(8,128)(2,1)S(1)}, bf16[64,1536]{1,0:T(8,128)(2,1)S(1)}, u32[]{:S(2)}, u32[]{:S(2)}) collective-permute-start(bf16[64,1536]{1,0:T(8,128)(2,1)S(1)} %get-tuple-element.20), channel_id=1, source_target_pairs={{0,64},{64,128},{128,0},{192,256},{256,320},{320,192},{384,448},{4... | collective-permute-start | bytes 589832 | tf_op jit(solution)/shard_map/ppermute | solution.py:187
  32.0 5.6 %collective-permute-start.1 = (bf16[64,1536]{1,0:T(8,128)(2,1)S(1)}, bf16[64,1536]{1,0:T(8,128)(2,1)S(1)}, u32[]{:S(2)}, u32[]{:S(2)}) collective-permute-start(bf16[64,1536]{1,0:T(8,128)(2,1)S(1)} %get-tuple-element.21), channel_id=1, source_target_pairs={{0,128},{64,0},{128,64},{192,320},{256,192},{320,256},{384,512},{4... | collective-permute-start | bytes 589832 | tf_op jit(solution)/shard_map/ppermute | solution.py:187
  37.5 3.4 %collective-permute-done.refs_1_ = bf16[64,1536]{1,0:T(8,128)(2,1)S(1)} collective-permute-done((bf16[64,1536]{1,0:T(8,128)(2,1)S(1)}, bf16[64,1536]{1,0:T(8,128)(2,1)S(1)}, u32[]{:S(2)}, u32[]{:S(2)}) %collective-permute-start) | collective-permute-done | bytes 196640 | tf_op jit(solution)/shard_map/ppermute | solution.py:187
  41.0 14.7 %collective-permute-done.1.refs_2_ = bf16[64,1536]{1,0:T(8,128)(2,1)S(1)} collective-permute-done((bf16[64,1536]{1,0:T(8,128)(2,1)S(1)}, bf16[64,1536]{1,0:T(8,128)(2,1)S(1)}, u32[]{:S(2)}, u32[]{:S(2)}) %collective-permute-start.1) | collective-permute-done | bytes 196640 | tf_op jit(solution)/shard_map/ppermute | solution.py:187
  55.7 0.7 shard_map.48
  56.4 18.3 %all-gather = bf16[256,1536]{1,0:T(8,128)(2,1)S(1)} all-gather(bf16[64,1536]{1,0:T(8,128)(2,1)S(1)} %shard_map.48), channel_id=2, replica_groups={{0,16,32,48},{4,20,36,52},{8,24,40,56},{12,28,44,60},{1,17,33,49},{5,21..., dimensions={0}, use_global_device_ids=true | all-gather | bytes 983040 | tf_op jit(solution)/shard_map/all_gather | solution.py:189
  74.7 2.1 %collective-permute-start.6 = (bf16[4,64,1536]{2,1,0:T(8,128)(2,1)S(1)}, bf16[4,64,1536]{2,1,0:T(8,128)(2,1)S(1)}, u32[]{:S(2)}, u32[]{:S(2)}) collective-permute-start(bf16[4,64,1536]{2,1,0:T(8,128)(2,1)S(1)} %bitcast.3), channel_id=1, source_target_pairs={{0,8},{4,12},{8,0},{12,4},{16,24},{20,28},{24,16},{28,20},{32,40},... | collective-permute-start | bytes 2359304 | tf_op jit(solution)/shard_map/ppermute | solution.py:190
  76.8 0.0 collective-permute-done.2.sibling_ref
  76.9 0.0 copy-done
  76.9 3.2 %shard_map.49 = (bf16[64,3072]{1,0:T(8,128)(2,1)S(1)}, bf16[64,3072]{1,0:T(8,128)(2,1)S(1)}, bf16[64,3072]{1,0:T(8,128)(2,1)S(1)}, bf16[64,3072]{1,0:T(8,128)(2,1)S(1)}) custom-call(bf16[4,64,1536]{2,1,0:T(8,128)(2,1)S(1)} %bitcast.4, bf16[1536,1536]{1,0:T(8,128)(2,1)S(1)} %collective-permute-done.2.sibling_ref, bf16[1536,1536]{1,0:T(8,128)(2,1)S(1)} %copy-done), custom_call_target="tpu_custom_call" | custom-call | tf_op jit(solution)/shard_map/pallas_call | solution.py:118
  80.0 7.2 %collective-permute-start.3 = (bf16[64,3072]{1,0:T(8,128)(2,1)S(1)}, bf16[64,3072]{1,0:T(8,128)(2,1)S(1)}, u32[]{:S(2)}, u32[]{:S(2)}) collective-permute-start(bf16[64,3072]{1,0:T(8,128)(2,1)S(1)} %get-tuple-element.25), channel_id=1, source_target_pairs={{0,1},{4,135},{8,9},{12,143},{16,17},{20,151},{24,25},{28,159},{32... | collective-permute-start | bytes 1179656 | tf_op jit(solution)/shard_map/ppermute | solution.py:195
  87.3 1.9 %collective-permute-start.5 = (bf16[64,3072]{1,0:T(8,128)(2,1)S(1)}, bf16[64,3072]{1,0:T(8,128)(2,1)S(1)}, u32[]{:S(2)}, u32[]{:S(2)}) collective-permute-start(bf16[64,3072]{1,0:T(8,128)(2,1)S(1)} %get-tuple-element.26), channel_id=1, source_target_pairs={{0,131},{4,5},{8,139},{12,13},{16,147},{20,21},{24,155},{28,29},{3... | collective-permute-start | bytes 1179656 | tf_op jit(solution)/shard_map/ppermute | solution.py:196
  89.2 1.6 %collective-permute-done.6.rows_ref = bf16[4,64,1536]{2,1,0:T(8,128)(2,1)S(1)} collective-permute-done((bf16[4,64,1536]{2,1,0:T(8,128)(2,1)S(1)}, bf16[4,64,1536]{2,1,0:T(8,128)(2,1)S(1)}, u32[]{:S(2)}, u32[]{:S(2)}) %collective-permute-start.6) | collective-permute-done | bytes 786464 | tf_op jit(solution)/shard_map/ppermute | solution.py:190
  90.8 3.2 %shard_map.50 = (bf16[64,3072]{1,0:T(8,128)(2,1)S(1)}, bf16[64,3072]{1,0:T(8,128)(2,1)S(1)}, bf16[64,3072]{1,0:T(8,128)(2,1)S(1)}, bf16[64,3072]{1,0:T(8,128)(2,1)S(1)}) custom-call(bf16[4,64,1536]{2,1,0:T(8,128)(2,1)S(1)} %collective-permute-done.6.rows_ref, bf16[1536,1536]{1,0:T(8,128)(2,1)S(1)} %collective-permute-done.2.sibling_ref, ...), custom_call_target="tpu_custom_call" | custom-call | tf_op jit(solution)/shard_map/pallas_call | solution.py:118
  94.0 0.0 copy-start.1
  94.0 6.6 %collective-permute-start.7 = (bf16[64,3072]{1,0:T(8,128)(2,1)S(1)}, bf16[64,3072]{1,0:T(8,128)(2,1)S(1)}, u32[]{:S(2)}, u32[]{:S(2)}) collective-permute-start(bf16[64,3072]{1,0:T(8,128)(2,1)S(1)} %get-tuple-element.29), channel_id=1, source_target_pairs={{0,1},{4,135},{8,9},{12,143},{16,17},{20,151},{24,25},{28,159},{32... | collective-permute-start | bytes 1179656 | tf_op jit(solution)/shard_map/ppermute | solution.py:195
  100.6 1.9 %collective-permute-start.9 = (bf16[64,3072]{1,0:T(8,128)(2,1)S(1)}, bf16[64,3072]{1,0:T(8,128)(2,1)S(1)}, u32[]{:S(2)}, u32[]{:S(2)}) collective-permute-start(bf16[64,3072]{1,0:T(8,128)(2,1)S(1)} %get-tuple-element.30), channel_id=1, source_target_pairs={{0,131},{4,5},{8,139},{12,13},{16,147},{20,21},{24,155},{28,29},{3... | collective-permute-start | bytes 1179656 | tf_op jit(solution)/shard_map/ppermute | solution.py:196
  102.6 0.0 collective-permute-done.3
  102.6 0.1 add_convert_fusion.1
  102.7 4.6 %collective-permute-start.4 = (bf16[64,3072]{1,0:T(8,128)(2,1)S(1)}, bf16[64,3072]{1,0:T(8,128)(2,1)S(1)}, u32[]{:S(2)}, u32[]{:S(2)}) collective-permute-start(bf16[64,3072]{1,0:T(8,128)(2,1)S(1)} %add_convert_fusion.1), channel_id=1, source_target_pairs={{0,1},{4,135},{8,9},{12,143},{16,17},{20,151},{24,25},{28,159},{32... | collective-permute-start | bytes 1179656 | tf_op jit(solution)/shard_map/ppermute | solution.py:198
  107.2 0.0 collective-permute-done.7
  107.3 0.1 add_convert_fusion
  107.4 3.1 %collective-permute-start.8 = (bf16[64,3072]{1,0:T(8,128)(2,1)S(1)}, bf16[64,3072]{1,0:T(8,128)(2,1)S(1)}, u32[]{:S(2)}, u32[]{:S(2)}) collective-permute-start(bf16[64,3072]{1,0:T(8,128)(2,1)S(1)} %add_convert_fusion), channel_id=1, source_target_pairs={{0,1},{4,135},{8,9},{12,143},{16,17},{20,151},{24,25},{28,159},{32... | collective-permute-start | bytes 1179656 | tf_op jit(solution)/shard_map/ppermute | solution.py:198
  110.5 0.0 collective-permute-done.5.refs_2_
  110.5 2.7 %collective-permute-done.9.refs_5_ = bf16[64,3072]{1,0:T(8,128)(2,1)S(1)} collective-permute-done((bf16[64,3072]{1,0:T(8,128)(2,1)S(1)}, bf16[64,3072]{1,0:T(8,128)(2,1)S(1)}, u32[]{:S(2)}, u32[]{:S(2)}) %collective-permute-start.9) | collective-permute-done | bytes 393248 | tf_op jit(solution)/shard_map/ppermute | solution.py:196
  113.2 1.8 %collective-permute-done.4.refs_1_ = bf16[64,3072]{1,0:T(8,128)(2,1)S(1)} collective-permute-done((bf16[64,3072]{1,0:T(8,128)(2,1)S(1)}, bf16[64,3072]{1,0:T(8,128)(2,1)S(1)}, u32[]{:S(2)}, u32[]{:S(2)}) %collective-permute-start.4) | collective-permute-done | bytes 393248 | tf_op jit(solution)/shard_map/ppermute | solution.py:198
  115.0 5.4 %collective-permute-done.8.refs_4_ = bf16[64,3072]{1,0:T(8,128)(2,1)S(1)} collective-permute-done((bf16[64,3072]{1,0:T(8,128)(2,1)S(1)}, bf16[64,3072]{1,0:T(8,128)(2,1)S(1)}, u32[]{:S(2)}, u32[]{:S(2)}) %collective-permute-start.8) | collective-permute-done | bytes 393248 | tf_op jit(solution)/shard_map/ppermute | solution.py:198
  120.4 0.1 shard_map.52
  120.5 7.8 %collective-permute-start.10 = (bf16[2,4,16,1536]{3,2,1,0:T(8,128)(2,1)S(1)}, bf16[2,4,16,1536]{3,2,1,0:T(8,128)(2,1)S(1)}, u32[]{:S(2)}, u32[]{:S(2)}) collective-permute-start(bf16[2,4,16,1536]{3,2,1,0:T(8,128)(2,1)S(1)} %shard_map.52), channel_id=1, source_target_pairs={{0,4},{4,0},{8,12},{12,8},{16,20},{20,16},{24,28},{28,24},{32,36},... | collective-permute-start | bytes 1179656 | tf_op jit(solution)/shard_map/ppermute | solution.py:212
  128.3 0.0 copy-done.1
  128.3 0.8 shard_map.51
  129.1 0.5 collective-permute-done.10.other_ref
  129.6 1.0 shard_map.53
Async XLA Ops:
  0.0 76.9 %copy-start = (bf16[1536,1536]{1,0:T(8,128)(2,1)S(1)}, bf16[1536,1536]{1,0:T(8,128)(2,1)}, u32[]{:S(2)}) copy-start(bf16[1536,1536]{1,0:T(8,128)(2,1)} %own_hbm.3) | copy-start | bytes 14155780
  0.0 1.2 copy-start.2
  1.2 0.9 copy-start.3
  15.5 61.3 %collective-permute-start.2 = (bf16[1536,1536]{1,0:T(8,128)(2,1)}, bf16[1536,1536]{1,0:T(8,128)(2,1)S(1)}, u32[]{:S(2)}, u32[]{:S(2)}) collective-permute-start(bf16[1536,1536]{1,0:T(8,128)(2,1)} %own_hbm.3), channel_id=1, source_target_pairs={{0,4},{4,0},{8,12},{12,8},{16,20},{20,16},{24,28},{28,24},{32,36},... | collective-permute-start | bytes 14155784 | tf_op jit(solution)/shard_map/ppermute | solution.py:186
  26.9 14.1 %collective-permute-start = (bf16[64,1536]{1,0:T(8,128)(2,1)S(1)}, bf16[64,1536]{1,0:T(8,128)(2,1)S(1)}, u32[]{:S(2)}, u32[]{:S(2)}) collective-permute-start(bf16[64,1536]{1,0:T(8,128)(2,1)S(1)} %get-tuple-element.20), channel_id=1, source_target_pairs={{0,64},{64,128},{128,0},{192,256},{256,320},{320,192},{384,448},{4... | collective-permute-start | bytes 589832 | tf_op jit(solution)/shard_map/ppermute | solution.py:187
  32.0 23.7 %collective-permute-start.1 = (bf16[64,1536]{1,0:T(8,128)(2,1)S(1)}, bf16[64,1536]{1,0:T(8,128)(2,1)S(1)}, u32[]{:S(2)}, u32[]{:S(2)}) collective-permute-start(bf16[64,1536]{1,0:T(8,128)(2,1)S(1)} %get-tuple-element.21), channel_id=1, source_target_pairs={{0,128},{64,0},{128,64},{192,320},{256,192},{320,256},{384,512},{4... | collective-permute-start | bytes 589832 | tf_op jit(solution)/shard_map/ppermute | solution.py:187
  74.7 16.1 %collective-permute-start.6 = (bf16[4,64,1536]{2,1,0:T(8,128)(2,1)S(1)}, bf16[4,64,1536]{2,1,0:T(8,128)(2,1)S(1)}, u32[]{:S(2)}, u32[]{:S(2)}) collective-permute-start(bf16[4,64,1536]{2,1,0:T(8,128)(2,1)S(1)} %bitcast.3), channel_id=1, source_target_pairs={{0,8},{4,12},{8,0},{12,4},{16,24},{20,28},{24,16},{28,20},{32,40},... | collective-permute-start | bytes 2359304 | tf_op jit(solution)/shard_map/ppermute | solution.py:190
  80.0 22.5 %collective-permute-start.3 = (bf16[64,3072]{1,0:T(8,128)(2,1)S(1)}, bf16[64,3072]{1,0:T(8,128)(2,1)S(1)}, u32[]{:S(2)}, u32[]{:S(2)}) collective-permute-start(bf16[64,3072]{1,0:T(8,128)(2,1)S(1)} %get-tuple-element.25), channel_id=1, source_target_pairs={{0,1},{4,135},{8,9},{12,143},{16,17},{20,151},{24,25},{28,159},{32... | collective-permute-start | bytes 1179656 | tf_op jit(solution)/shard_map/ppermute | solution.py:195
  87.3 23.2 %collective-permute-start.5 = (bf16[64,3072]{1,0:T(8,128)(2,1)S(1)}, bf16[64,3072]{1,0:T(8,128)(2,1)S(1)}, u32[]{:S(2)}, u32[]{:S(2)}) collective-permute-start(bf16[64,3072]{1,0:T(8,128)(2,1)S(1)} %get-tuple-element.26), channel_id=1, source_target_pairs={{0,131},{4,5},{8,139},{12,13},{16,147},{20,21},{24,155},{28,29},{3... | collective-permute-start | bytes 1179656 | tf_op jit(solution)/shard_map/ppermute | solution.py:196
  94.0 34.3 %copy-start.1 = (bf16[256,1536]{1,0:T(8,128)(2,1)S(1)}, bf16[256,1536]{1,0:T(8,128)(2,1)}, u32[]{:S(2)}) copy-start(bf16[256,1536]{1,0:T(8,128)(2,1)} %param.7) | copy-start | bytes 2359300
  94.0 13.3 %collective-permute-start.7 = (bf16[64,3072]{1,0:T(8,128)(2,1)S(1)}, bf16[64,3072]{1,0:T(8,128)(2,1)S(1)}, u32[]{:S(2)}, u32[]{:S(2)}) collective-permute-start(bf16[64,3072]{1,0:T(8,128)(2,1)S(1)} %get-tuple-element.29), channel_id=1, source_target_pairs={{0,1},{4,135},{8,9},{12,143},{16,17},{20,151},{24,25},{28,159},{32... | collective-permute-start | bytes 1179656 | tf_op jit(solution)/shard_map/ppermute | solution.py:195
  100.6 12.5 %collective-permute-start.9 = (bf16[64,3072]{1,0:T(8,128)(2,1)S(1)}, bf16[64,3072]{1,0:T(8,128)(2,1)S(1)}, u32[]{:S(2)}, u32[]{:S(2)}) collective-permute-start(bf16[64,3072]{1,0:T(8,128)(2,1)S(1)} %get-tuple-element.30), channel_id=1, source_target_pairs={{0,131},{4,5},{8,139},{12,13},{16,147},{20,21},{24,155},{28,29},{3... | collective-permute-start | bytes 1179656 | tf_op jit(solution)/shard_map/ppermute | solution.py:196
  102.7 12.3 %collective-permute-start.4 = (bf16[64,3072]{1,0:T(8,128)(2,1)S(1)}, bf16[64,3072]{1,0:T(8,128)(2,1)S(1)}, u32[]{:S(2)}, u32[]{:S(2)}) collective-permute-start(bf16[64,3072]{1,0:T(8,128)(2,1)S(1)} %add_convert_fusion.1), channel_id=1, source_target_pairs={{0,1},{4,135},{8,9},{12,143},{16,17},{20,151},{24,25},{28,159},{32... | collective-permute-start | bytes 1179656 | tf_op jit(solution)/shard_map/ppermute | solution.py:198
  107.4 13.0 %collective-permute-start.8 = (bf16[64,3072]{1,0:T(8,128)(2,1)S(1)}, bf16[64,3072]{1,0:T(8,128)(2,1)S(1)}, u32[]{:S(2)}, u32[]{:S(2)}) collective-permute-start(bf16[64,3072]{1,0:T(8,128)(2,1)S(1)} %add_convert_fusion), channel_id=1, source_target_pairs={{0,1},{4,135},{8,9},{12,143},{16,17},{20,151},{24,25},{28,159},{32... | collective-permute-start | bytes 1179656 | tf_op jit(solution)/shard_map/ppermute | solution.py:198
  120.5 9.1 %collective-permute-start.10 = (bf16[2,4,16,1536]{3,2,1,0:T(8,128)(2,1)S(1)}, bf16[2,4,16,1536]{3,2,1,0:T(8,128)(2,1)S(1)}, u32[]{:S(2)}, u32[]{:S(2)}) collective-permute-start(bf16[2,4,16,1536]{3,2,1,0:T(8,128)(2,1)S(1)} %shard_map.52), channel_id=1, source_target_pairs={{0,4},{4,0},{8,12},{12,8},{16,20},{20,16},{24,28},{28,24},{32,36},... | collective-permute-start | bytes 1179656 | tf_op jit(solution)/shard_map/ppermute | solution.py:212

commit v4 on v3

--- a/solution.py
+++ b/solution.py
@@ -88,10 +88,7 @@
         out_ref[rows] = block
 
 
-def product_kernel(rows_ref, sibling_ref, own_hbm, *refs):
-    out_refs, (own_ref, sem) = refs[:-2], refs[-2:]
-    copy = pltpu.make_async_copy(own_hbm, own_ref, sem)
-    copy.start()
+def product_kernel(rows_ref, sibling_ref, own_ref, *out_refs):
     hidden, width = sibling_ref.shape
     rows = jnp.concatenate(
         [rows_ref[:, s * ROWS:(s + 1) * ROWS].reshape(-1, width) for s in range(SLOTS)], axis=0
@@ -108,7 +105,6 @@
                 out_ref[:, start + tile:start + tile + HIDDEN_TILE] = value[s * size:(s + 1) * size]
 
     run(sibling_ref, hidden)
-    copy.wait()
     run(own_ref, 0)
 
 
@@ -117,10 +113,9 @@
     vmem = pl.BlockSpec(memory_space=pltpu.VMEM)
     return pl.pallas_call(
         product_kernel,
-        in_specs=[vmem] * 2 + [pl.BlockSpec(memory_space=pl.ANY)],
+        in_specs=[vmem] * 3,
         out_specs=[vmem] * SLOTS,
         out_shape=[jax.ShapeDtypeStruct((HALF * ROWS, 2 * hidden), jnp.bfloat16)] * SLOTS,
-        scratch_shapes=[pltpu.VMEM((hidden, width), jnp.bfloat16), pltpu.SemaphoreType.DMA],
         compiler_params=params(),
     )(blocks, sibling, own)
 
@@ -179,11 +174,10 @@
             compiler_params=params(),
         )(lang_rank, *values)
 
+    sibling = lax.ppermute(weight_down, "wout", CORE_SWAP)
     held = move(rank_blocks_kernel, (NX, NZH * ROWS), returned)
     held = lax.all_to_all(held, "dp", 0, 0, axis_index_groups=X_GROUPS)
     windows = move(window_blocks_kernel, (SLOTS * ROWS,), held, count=NZH)
-    weight_sent, _ = lax.optimization_barrier((weight_down, windows[1]))
-    sibling = lax.ppermute(weight_sent, "wout", CORE_SWAP)
     windows = [windows[0]] + [lax.ppermute(windows[j], "dp", zh_perm(j)) for j in range(1, NZH)]
     window = move(window_pick_kernel, (SLOTS * ROWS,), *windows)
     near = lax.all_gather(window, "wout", axis_index_groups=PARITY_GROUPS)

time: 131 us -> 130 us (level)
  waiting for transfers between devices: 30.2 us -> 27.1 us
  starting transfers between devices: 57.2 us -> 60.3 us
    ppermute x2, starting transfers between devices: 13.8 us -> 16.5 us  [local(): far = lax.ppermute(far, RING, ring_perm(1))]
    ppermute x2, waiting for transfers between devices: 18.2 us -> 16.3 us  [local(): lax.ppermute(windows[j], 'dp', zh_perm(j))]
    ppermute x2, starting transfers between devices: 10.6 us -> 9.19 us  [local(): lax.ppermute(windows[j], 'dp', zh_perm(j))]
    ppermute x1, starting transfers between devices: 11.3 us -> 12.7 us  [local(): sibling = lax.ppermute(weight_down, 'wout', CORE_SWAP)]
    ppermute x1, waiting for transfers between devices: 1.63 us -> 0.32 us  [local(): others = lax.ppermute(near, 'wout', PAIR_SWAP)]
where the time goes in v4:
time: 130 us
  starting transfers between devices  60.3 us (46%)
  blocking collectives  30.8 us (24%)
  waiting for transfers between devices  27.1 us (21%)
  Pallas kernels  9.29 us (7%)
  local copies, waits for them, and re-layouts  1.72 us (1%)
    all_gather x1, blocking collectives, local(): near = lax.all_gather(window, 'wout', axis_index_groups=PARITY_GROUPS)  18 us
    ppermute x2, starting transfers between devices, local(): far = lax.ppermute(far, RING, ring_perm(1))  16.5 us
    ppermute x2, waiting for transfers between devices, local(): lax.ppermute(windows[j], 'dp', zh_perm(j))  16.3 us
    all_to_all x1, blocking collectives, local(): held = lax.all_to_all(held, 'dp', 0, 0, axis_index_groups=X_GROUPS)  12.7 us
    ppermute x1, starting transfers between devices, local(): sibling = lax.ppermute(weight_down, 'wout', CORE_SWAP)  12.7 us
    ppermute x2, starting transfers between devices, local(): lax.ppermute(windows[j], 'dp', zh_perm(j))  9.19 us
    ppermute x1, starting transfers between devices, local(): other = lax.ppermute(sent, 'wout', CORE_SWAP)  7.77 us
    ppermute x2, starting transfers between devices, local(): parts += [mine, lax.ppermute(ahead, RING, ring_perm(1)), behind]  7.66 us
  transfers between devices with their start and end apart: 11, of which 7 were waited for; matrix products, arithmetic and copies ran while one was open for 0% of the time, Pallas kernels for 6%

profile of v4, /device:TPU:1, one launch (start us, length us, event | category | flops | bytes accessed | tf_op | source)
XLA Modules:
  0.0 129.5 jit_solution(14498425619395993062)
XLA Ops:
  0.0 0.0 copy-start
  0.0 12.7 %collective-permute-start.2 = (bf16[1536,1536]{1,0:T(8,128)(2,1)}, bf16[1536,1536]{1,0:T(8,128)(2,1)S(1)}, u32[]{:S(2)}, u32[]{:S(2)}) collective-permute-start(bf16[1536,1536]{1,0:T(8,128)(2,1)} %own_ref.3), channel_id=1, source_target_pairs={{0,4},{4,0},{8,12},{12,8},{16,20},{20,16},{24,28},{28,24},{32,36},... | collective-permute-start | bytes 14155784 | tf_op jit(solution)/shard_map/ppermute | solution.py:177
  12.7 0.0 copy-start.2
  12.7 1.1 copy-done.2
  13.8 0.0 copy-start.3
  13.8 0.7 copy-done.3
  14.4 0.6 shard_map.46
  15.1 12.7 %all_to_all.5.in_ref = bf16[4,48,1536]{2,1,0:T(8,128)(2,1)S(1)} all-to-all(bf16[4,48,1536]{2,1,0:T(8,128)(2,1)S(1)} %shard_map.46), channel_id=1, replica_groups={{0,192,384,576},{64,256,448,640},{128,320,512,704},{1,193,385,577},{65,..., dimensions={0} | all-to-all | bytes 1179648 | tf_op jit(solution)/shard_map/all_to_all | solution.py:179
  27.8 0.8 shard_map.47
  28.6 2.4 %collective-permute-start = (bf16[64,1536]{1,0:T(8,128)(2,1)S(1)}, bf16[64,1536]{1,0:T(8,128)(2,1)S(1)}, u32[]{:S(2)}, u32[]{:S(2)}) collective-permute-start(bf16[64,1536]{1,0:T(8,128)(2,1)S(1)} %get-tuple-element.19), channel_id=1, source_target_pairs={{0,64},{64,128},{128,0},{192,256},{256,320},{320,192},{384,448},{4... | collective-permute-start | bytes 589832 | tf_op jit(solution)/shard_map/ppermute | solution.py:181
  31.0 6.7 %collective-permute-start.1 = (bf16[64,1536]{1,0:T(8,128)(2,1)S(1)}, bf16[64,1536]{1,0:T(8,128)(2,1)S(1)}, u32[]{:S(2)}, u32[]{:S(2)}) collective-permute-start(bf16[64,1536]{1,0:T(8,128)(2,1)S(1)} %get-tuple-element.20), channel_id=1, source_target_pairs={{0,128},{64,0},{128,64},{192,320},{256,192},{320,256},{384,512},{4... | collective-permute-start | bytes 589832 | tf_op jit(solution)/shard_map/ppermute | solution.py:181
  37.8 2.4 %collective-permute-done.refs_1_ = bf16[64,1536]{1,0:T(8,128)(2,1)S(1)} collective-permute-done((bf16[64,1536]{1,0:T(8,128)(2,1)S(1)}, bf16[64,1536]{1,0:T(8,128)(2,1)S(1)}, u32[]{:S(2)}, u32[]{:S(2)}) %collective-permute-start) | collective-permute-done | bytes 196640 | tf_op jit(solution)/shard_map/ppermute | solution.py:181
  40.2 13.9 %collective-permute-done.1.refs_2_ = bf16[64,1536]{1,0:T(8,128)(2,1)S(1)} collective-permute-done((bf16[64,1536]{1,0:T(8,128)(2,1)S(1)}, bf16[64,1536]{1,0:T(8,128)(2,1)S(1)}, u32[]{:S(2)}, u32[]{:S(2)}) %collective-permute-start.1) | collective-permute-done | bytes 196640 | tf_op jit(solution)/shard_map/ppermute | solution.py:181
  54.1 0.7 shard_map.48
  54.8 18.0 %all-gather = bf16[256,1536]{1,0:T(8,128)(2,1)S(1)} all-gather(bf16[64,1536]{1,0:T(8,128)(2,1)S(1)} %shard_map.48), channel_id=2, replica_groups={{0,16,32,48},{4,20,36,52},{8,24,40,56},{12,28,44,60},{1,17,33,49},{5,21..., dimensions={0}, use_global_device_ids=true | all-gather | bytes 983040 | tf_op jit(solution)/shard_map/all_gather | solution.py:183
  72.8 2.7 %collective-permute-start.6 = (bf16[4,64,1536]{2,1,0:T(8,128)(2,1)S(1)}, bf16[4,64,1536]{2,1,0:T(8,128)(2,1)S(1)}, u32[]{:S(2)}, u32[]{:S(2)}) collective-permute-start(bf16[4,64,1536]{2,1,0:T(8,128)(2,1)S(1)} %bitcast.3), channel_id=1, source_target_pairs={{0,8},{4,12},{8,0},{12,4},{16,24},{20,28},{24,16},{28,20},{32,40},... | collective-permute-start | bytes 2359304 | tf_op jit(solution)/shard_map/ppermute | solution.py:184
  75.5 0.0 collective-permute-done.2.sibling_ref
  75.5 0.0 copy-done
  75.6 2.6 %shard_map.49 = (bf16[64,3072]{1,0:T(8,128)(2,1)S(1)}, bf16[64,3072]{1,0:T(8,128)(2,1)S(1)}, bf16[64,3072]{1,0:T(8,128)(2,1)S(1)}, bf16[64,3072]{1,0:T(8,128)(2,1)S(1)}) custom-call(bf16[4,64,1536]{2,1,0:T(8,128)(2,1)S(1)} %bitcast.4, bf16[1536,1536]{1,0:T(8,128)(2,1)S(1)} %collective-permute-done.2.sibling_ref, bf16[1536,1536]{1,0:T(8,128)(2,1)S(1)} %copy-done), custom_call_target="tpu_custom_call" | custom-call | tf_op jit(solution)/shard_map/pallas_call | solution.py:114
  78.2 8.1 %collective-permute-start.3 = (bf16[64,3072]{1,0:T(8,128)(2,1)S(1)}, bf16[64,3072]{1,0:T(8,128)(2,1)S(1)}, u32[]{:S(2)}, u32[]{:S(2)}) collective-permute-start(bf16[64,3072]{1,0:T(8,128)(2,1)S(1)} %get-tuple-element.23), channel_id=1, source_target_pairs={{0,1},{4,135},{8,9},{12,143},{16,17},{20,151},{24,25},{28,159},{32... | collective-permute-start | bytes 1179656 | tf_op jit(solution)/shard_map/ppermute | solution.py:189
  86.3 1.9 %collective-permute-start.5 = (bf16[64,3072]{1,0:T(8,128)(2,1)S(1)}, bf16[64,3072]{1,0:T(8,128)(2,1)S(1)}, u32[]{:S(2)}, u32[]{:S(2)}) collective-permute-start(bf16[64,3072]{1,0:T(8,128)(2,1)S(1)} %get-tuple-element.24), channel_id=1, source_target_pairs={{0,131},{4,5},{8,139},{12,13},{16,147},{20,21},{24,155},{28,29},{3... | collective-permute-start | bytes 1179656 | tf_op jit(solution)/shard_map/ppermute | solution.py:190
  88.2 0.3 collective-permute-done.6.rows_ref
  88.5 2.6 %shard_map.50 = (bf16[64,3072]{1,0:T(8,128)(2,1)S(1)}, bf16[64,3072]{1,0:T(8,128)(2,1)S(1)}, bf16[64,3072]{1,0:T(8,128)(2,1)S(1)}, bf16[64,3072]{1,0:T(8,128)(2,1)S(1)}) custom-call(bf16[4,64,1536]{2,1,0:T(8,128)(2,1)S(1)} %collective-permute-done.6.rows_ref, bf16[1536,1536]{1,0:T(8,128)(2,1)S(1)} %collective-permute-done.2.sibling_ref, ...), custom_call_target="tpu_custom_call" | custom-call | tf_op jit(solution)/shard_map/pallas_call | solution.py:114
  91.2 0.0 copy-start.1
  91.2 8.4 %collective-permute-start.7 = (bf16[64,3072]{1,0:T(8,128)(2,1)S(1)}, bf16[64,3072]{1,0:T(8,128)(2,1)S(1)}, u32[]{:S(2)}, u32[]{:S(2)}) collective-permute-start(bf16[64,3072]{1,0:T(8,128)(2,1)S(1)} %get-tuple-element.27), channel_id=1, source_target_pairs={{0,1},{4,135},{8,9},{12,143},{16,17},{20,151},{24,25},{28,159},{32... | collective-permute-start | bytes 1179656 | tf_op jit(solution)/shard_map/ppermute | solution.py:189
  99.6 1.9 %collective-permute-start.9 = (bf16[64,3072]{1,0:T(8,128)(2,1)S(1)}, bf16[64,3072]{1,0:T(8,128)(2,1)S(1)}, u32[]{:S(2)}, u32[]{:S(2)}) collective-permute-start(bf16[64,3072]{1,0:T(8,128)(2,1)S(1)} %get-tuple-element.28), channel_id=1, source_target_pairs={{0,131},{4,5},{8,139},{12,13},{16,147},{20,21},{24,155},{28,29},{3... | collective-permute-start | bytes 1179656 | tf_op jit(solution)/shard_map/ppermute | solution.py:190
  101.5 0.0 collective-permute-done.3
  101.5 0.1 add_convert_fusion.1
  101.6 4.6 %collective-permute-start.4 = (bf16[64,3072]{1,0:T(8,128)(2,1)S(1)}, bf16[64,3072]{1,0:T(8,128)(2,1)S(1)}, u32[]{:S(2)}, u32[]{:S(2)}) collective-permute-start(bf16[64,3072]{1,0:T(8,128)(2,1)S(1)} %add_convert_fusion.1), channel_id=1, source_target_pairs={{0,1},{4,135},{8,9},{12,143},{16,17},{20,151},{24,25},{28,159},{32... | collective-permute-start | bytes 1179656 | tf_op jit(solution)/shard_map/ppermute | solution.py:192
  106.2 0.0 collective-permute-done.7
  106.2 0.1 add_convert_fusion
  106.3 3.1 %collective-permute-start.8 = (bf16[64,3072]{1,0:T(8,128)(2,1)S(1)}, bf16[64,3072]{1,0:T(8,128)(2,1)S(1)}, u32[]{:S(2)}, u32[]{:S(2)}) collective-permute-start(bf16[64,3072]{1,0:T(8,128)(2,1)S(1)} %add_convert_fusion), channel_id=1, source_target_pairs={{0,1},{4,135},{8,9},{12,143},{16,17},{20,151},{24,25},{28,159},{32... | collective-permute-start | bytes 1179656 | tf_op jit(solution)/shard_map/ppermute | solution.py:192
  109.4 0.0 collective-permute-done.5.refs_2_
  109.4 3.2 %collective-permute-done.9.refs_5_ = bf16[64,3072]{1,0:T(8,128)(2,1)S(1)} collective-permute-done((bf16[64,3072]{1,0:T(8,128)(2,1)S(1)}, bf16[64,3072]{1,0:T(8,128)(2,1)S(1)}, u32[]{:S(2)}, u32[]{:S(2)}) %collective-permute-start.9) | collective-permute-done | bytes 393248 | tf_op jit(solution)/shard_map/ppermute | solution.py:190
  112.6 1.1 collective-permute-done.4.refs_1_
  113.8 5.6 %collective-permute-done.8.refs_4_ = bf16[64,3072]{1,0:T(8,128)(2,1)S(1)} collective-permute-done((bf16[64,3072]{1,0:T(8,128)(2,1)S(1)}, bf16[64,3072]{1,0:T(8,128)(2,1)S(1)}, u32[]{:S(2)}, u32[]{:S(2)}) %collective-permute-start.8) | collective-permute-done | bytes 393248 | tf_op jit(solution)/shard_map/ppermute | solution.py:192
  119.3 0.1 shard_map.52
  119.5 7.8 %collective-permute-start.10 = (bf16[2,4,16,1536]{3,2,1,0:T(8,128)(2,1)S(1)}, bf16[2,4,16,1536]{3,2,1,0:T(8,128)(2,1)S(1)}, u32[]{:S(2)}, u32[]{:S(2)}) collective-permute-start(bf16[2,4,16,1536]{3,2,1,0:T(8,128)(2,1)S(1)} %shard_map.52), channel_id=1, source_target_pairs={{0,4},{4,0},{8,12},{12,8},{16,20},{20,16},{24,28},{28,24},{32,36},... | collective-permute-start | bytes 1179656 | tf_op jit(solution)/shard_map/ppermute | solution.py:206
  127.2 0.0 copy-done.1
  127.2 0.8 shard_map.51
  128.0 0.5 collective-permute-done.10.other_ref
  128.6 1.0 shard_map.53
Async XLA Ops:
  0.0 75.5 %copy-start = (bf16[1536,1536]{1,0:T(8,128)(2,1)S(1)}, bf16[1536,1536]{1,0:T(8,128)(2,1)}, u32[]{:S(2)}) copy-start(bf16[1536,1536]{1,0:T(8,128)(2,1)} %own_ref.3) | copy-start | bytes 14155780
  0.0 75.5 %collective-permute-start.2 = (bf16[1536,1536]{1,0:T(8,128)(2,1)}, bf16[1536,1536]{1,0:T(8,128)(2,1)S(1)}, u32[]{:S(2)}, u32[]{:S(2)}) collective-permute-start(bf16[1536,1536]{1,0:T(8,128)(2,1)} %own_ref.3), channel_id=1, source_target_pairs={{0,4},{4,0},{8,12},{12,8},{16,20},{20,16},{24,28},{28,24},{32,36},... | collective-permute-start | bytes 14155784 | tf_op jit(solution)/shard_map/ppermute | solution.py:177
  12.7 1.1 copy-start.2
  13.8 0.7 copy-start.3
  28.6 11.6 %collective-permute-start = (bf16[64,1536]{1,0:T(8,128)(2,1)S(1)}, bf16[64,1536]{1,0:T(8,128)(2,1)S(1)}, u32[]{:S(2)}, u32[]{:S(2)}) collective-permute-start(bf16[64,1536]{1,0:T(8,128)(2,1)S(1)} %get-tuple-element.19), channel_id=1, source_target_pairs={{0,64},{64,128},{128,0},{192,256},{256,320},{320,192},{384,448},{4... | collective-permute-start | bytes 589832 | tf_op jit(solution)/shard_map/ppermute | solution.py:181
  31.0 23.1 %collective-permute-start.1 = (bf16[64,1536]{1,0:T(8,128)(2,1)S(1)}, bf16[64,1536]{1,0:T(8,128)(2,1)S(1)}, u32[]{:S(2)}, u32[]{:S(2)}) collective-permute-start(bf16[64,1536]{1,0:T(8,128)(2,1)S(1)} %get-tuple-element.20), channel_id=1, source_target_pairs={{0,128},{64,0},{128,64},{192,320},{256,192},{320,256},{384,512},{4... | collective-permute-start | bytes 589832 | tf_op jit(solution)/shard_map/ppermute | solution.py:181
  72.8 15.7 %collective-permute-start.6 = (bf16[4,64,1536]{2,1,0:T(8,128)(2,1)S(1)}, bf16[4,64,1536]{2,1,0:T(8,128)(2,1)S(1)}, u32[]{:S(2)}, u32[]{:S(2)}) collective-permute-start(bf16[4,64,1536]{2,1,0:T(8,128)(2,1)S(1)} %bitcast.3), channel_id=1, source_target_pairs={{0,8},{4,12},{8,0},{12,4},{16,24},{20,28},{24,16},{28,20},{32,40},... | collective-permute-start | bytes 2359304 | tf_op jit(solution)/shard_map/ppermute | solution.py:184
  78.2 23.3 %collective-permute-start.3 = (bf16[64,3072]{1,0:T(8,128)(2,1)S(1)}, bf16[64,3072]{1,0:T(8,128)(2,1)S(1)}, u32[]{:S(2)}, u32[]{:S(2)}) collective-permute-start(bf16[64,3072]{1,0:T(8,128)(2,1)S(1)} %get-tuple-element.23), channel_id=1, source_target_pairs={{0,1},{4,135},{8,9},{12,143},{16,17},{20,151},{24,25},{28,159},{32... | collective-permute-start | bytes 1179656 | tf_op jit(solution)/shard_map/ppermute | solution.py:189
  86.3 23.1 %collective-permute-start.5 = (bf16[64,3072]{1,0:T(8,128)(2,1)S(1)}, bf16[64,3072]{1,0:T(8,128)(2,1)S(1)}, u32[]{:S(2)}, u32[]{:S(2)}) collective-permute-start(bf16[64,3072]{1,0:T(8,128)(2,1)S(1)} %get-tuple-element.24), channel_id=1, source_target_pairs={{0,131},{4,5},{8,139},{12,13},{16,147},{20,21},{24,155},{28,29},{3... | collective-permute-start | bytes 1179656 | tf_op jit(solution)/shard_map/ppermute | solution.py:190
  91.2 36.1 %copy-start.1 = (bf16[256,1536]{1,0:T(8,128)(2,1)S(1)}, bf16[256,1536]{1,0:T(8,128)(2,1)}, u32[]{:S(2)}) copy-start(bf16[256,1536]{1,0:T(8,128)(2,1)} %param.7) | copy-start | bytes 2359300
  91.2 15.0 %collective-permute-start.7 = (bf16[64,3072]{1,0:T(8,128)(2,1)S(1)}, bf16[64,3072]{1,0:T(8,128)(2,1)S(1)}, u32[]{:S(2)}, u32[]{:S(2)}) collective-permute-start(bf16[64,3072]{1,0:T(8,128)(2,1)S(1)} %get-tuple-element.27), channel_id=1, source_target_pairs={{0,1},{4,135},{8,9},{12,143},{16,17},{20,151},{24,25},{28,159},{32... | collective-permute-start | bytes 1179656 | tf_op jit(solution)/shard_map/ppermute | solution.py:189
  99.6 13.1 %collective-permute-start.9 = (bf16[64,3072]{1,0:T(8,128)(2,1)S(1)}, bf16[64,3072]{1,0:T(8,128)(2,1)S(1)}, u32[]{:S(2)}, u32[]{:S(2)}) collective-permute-start(bf16[64,3072]{1,0:T(8,128)(2,1)S(1)} %get-tuple-element.28), channel_id=1, source_target_pairs={{0,131},{4,5},{8,139},{12,13},{16,147},{20,21},{24,155},{28,29},{3... | collective-permute-start | bytes 1179656 | tf_op jit(solution)/shard_map/ppermute | solution.py:190
  101.6 12.1 %collective-permute-start.4 = (bf16[64,3072]{1,0:T(8,128)(2,1)S(1)}, bf16[64,3072]{1,0:T(8,128)(2,1)S(1)}, u32[]{:S(2)}, u32[]{:S(2)}) collective-permute-start(bf16[64,3072]{1,0:T(8,128)(2,1)S(1)} %add_convert_fusion.1), channel_id=1, source_target_pairs={{0,1},{4,135},{8,9},{12,143},{16,17},{20,151},{24,25},{28,159},{32... | collective-permute-start | bytes 1179656 | tf_op jit(solution)/shard_map/ppermute | solution.py:192
  106.3 13.0 %collective-permute-start.8 = (bf16[64,3072]{1,0:T(8,128)(2,1)S(1)}, bf16[64,3072]{1,0:T(8,128)(2,1)S(1)}, u32[]{:S(2)}, u32[]{:S(2)}) collective-permute-start(bf16[64,3072]{1,0:T(8,128)(2,1)S(1)} %add_convert_fusion), channel_id=1, source_target_pairs={{0,1},{4,135},{8,9},{12,143},{16,17},{20,151},{24,25},{28,159},{32... | collective-permute-start | bytes 1179656 | tf_op jit(solution)/shard_map/ppermute | solution.py:192
  119.5 9.1 %collective-permute-start.10 = (bf16[2,4,16,1536]{3,2,1,0:T(8,128)(2,1)S(1)}, bf16[2,4,16,1536]{3,2,1,0:T(8,128)(2,1)S(1)}, u32[]{:S(2)}, u32[]{:S(2)}) collective-permute-start(bf16[2,4,16,1536]{3,2,1,0:T(8,128)(2,1)S(1)} %shard_map.52), channel_id=1, source_target_pairs={{0,4},{4,0},{8,12},{12,8},{16,20},{20,16},{24,28},{28,24},{32,36},... | collective-permute-start | bytes 1179656 | tf_op jit(solution)/shard_map/ppermute | solution.py:206

commit v5 on v4

--- a/solution.py
+++ b/solution.py
@@ -1,3 +1,5 @@
+import functools
+
 import jax
 import jax.numpy as jnp
 from jax import lax
@@ -17,7 +19,6 @@
 X_GROUPS = [[x * NZH + z for x in range(NX)] for z in range(NZH)]
 PARITY_GROUPS = [[y * 2 + c for y in range(p, NY, 2)] for p in range(2) for c in range(2)]
 CORE_SWAP = [(w, w ^ 1) for w in range(2 * NY)]
-PAIR_SWAP = [(w, w ^ 2) for w in range(2 * NY)]
 RING = ("dp", "wout", "win")
 
 
@@ -39,6 +40,10 @@
 
 def zh_perm(step):
     return [(x * NZH + z, x * NZH + (z + step) % NZH) for x in range(NX) for z in range(NZH)]
+
+
+def y_perm(step):
+    return [(y * 2 + c, (y + step) % NY * 2 + c) for y in range(NY) for c in range(2)]
 
 
 def params():
@@ -88,10 +93,15 @@
         out_ref[rows] = block
 
 
-def product_kernel(rows_ref, sibling_ref, own_ref, *out_refs):
+def product_kernel(count, *refs):
+    rows_refs, (sibling_ref, own_ref), out_refs = refs[:count], refs[count:count + 2], refs[count + 2:]
     hidden, width = sibling_ref.shape
     rows = jnp.concatenate(
-        [rows_ref[:, s * ROWS:(s + 1) * ROWS].reshape(-1, width) for s in range(SLOTS)], axis=0
+        [
+            ref[:, s * ROWS:(s + 1) * ROWS].reshape(-1, width)
+            for s in range(SLOTS) for ref in rows_refs
+        ],
+        axis=0,
     )
 
     def run(weight_ref, start):
@@ -112,12 +122,12 @@
     hidden, width = own.shape
     vmem = pl.BlockSpec(memory_space=pltpu.VMEM)
     return pl.pallas_call(
-        product_kernel,
-        in_specs=[vmem] * 3,
+        functools.partial(product_kernel, len(blocks)),
+        in_specs=[vmem] * (len(blocks) + 2),
         out_specs=[vmem] * SLOTS,
         out_shape=[jax.ShapeDtypeStruct((HALF * ROWS, 2 * hidden), jnp.bfloat16)] * SLOTS,
         compiler_params=params(),
-    )(blocks, sibling, own)
+    )(*blocks, sibling, own)
 
 
 def parity_and_core():
@@ -181,10 +191,13 @@
     windows = [windows[0]] + [lax.ppermute(windows[j], "dp", zh_perm(j)) for j in range(1, NZH)]
     window = move(window_pick_kernel, (SLOTS * ROWS,), *windows)
     near = lax.all_gather(window, "wout", axis_index_groups=PARITY_GROUPS)
-    others = lax.ppermute(near, "wout", PAIR_SWAP)
+    others = [
+        lax.ppermute(near[:HALF // 2], "wout", y_perm(1)),
+        lax.ppermute(near[HALF // 2:], "wout", y_perm(-1)),
+    ]
 
     parts = []
-    for blocks in (near, others):
+    for blocks in ([near], others):
         far, ahead, behind, mine = product(blocks, weight_down, sibling)
         far = lax.ppermute(far, RING, ring_perm(1))
         behind = lax.ppermute(behind, RING, ring_perm(-1))

time: 130 us -> 130 us (level)
  waiting for transfers between devices: 27.1 us -> 24.9 us
  starting transfers between devices: 60.3 us -> 62.4 us
    ppermute x1 -> x2, starting transfers between devices: 2.67 us -> 6.49 us  [the longest x1 3.81 us: local(): lax.ppermute(near[HALF // 2:], 'wout', y_perm(-1))]
    ppermute x2, starting transfers between devices: 16.5 us -> 12.9 us  [local(): far = lax.ppermute(far, RING, ring_perm(1))]
    ppermute x2, waiting for transfers between devices: 3.25 us -> 0.52 us  [local(): behind = lax.ppermute(behind, RING, ring_perm(-1))]
    ppermute x2, starting transfers between devices: 7.66 us -> 9.6 us  [local(): parts += [mine, lax.ppermute(ahead, RING, ring_perm(1)), behind]]
  transfers between devices with their start and end apart: 11 -> 12, of which waited for: 7 -> 7; matrix products, arithmetic and copies ran while one was open for 0% -> 0% of each run, Pallas kernels for 6% -> 6%
where the time goes in v5:
time: 130 us
  starting transfers between devices  62.4 us (48%)
  blocking collectives  30.8 us (24%)
  waiting for transfers between devices  24.9 us (19%)
  Pallas kernels  9.29 us (7%)
  local copies, waits for them, and re-layouts  1.77 us (1%)
    all_gather x1, blocking collectives, local(): near = lax.all_gather(window, 'wout', axis_index_groups=PARITY_GROUPS)  18 us
    ppermute x2, waiting for transfers between devices, local(): lax.ppermute(windows[j], 'dp', zh_perm(j))  16.3 us
    ppermute x2, starting transfers between devices, local(): far = lax.ppermute(far, RING, ring_perm(1))  12.9 us
    all_to_all x1, blocking collectives, local(): held = lax.all_to_all(held, 'dp', 0, 0, axis_index_groups=X_GROUPS)  12.7 us
    ppermute x1, starting transfers between devices, local(): sibling = lax.ppermute(weight_down, 'wout', CORE_SWAP)  12.7 us
    ppermute x2, starting transfers between devices, local(): parts += [mine, lax.ppermute(ahead, RING, ring_perm(1)), behind]  9.6 us
    ppermute x2, starting transfers between devices, local(): lax.ppermute(windows[j], 'dp', zh_perm(j))  9.19 us
    ppermute x1, starting transfers between devices, local(): other = lax.ppermute(sent, 'wout', CORE_SWAP)  7.7 us
  transfers between devices with their start and end apart: 12, of which 7 were waited for; matrix products, arithmetic and copies ran while one was open for 0% of the time, Pallas kernels for 6%

profile of v5, /device:TPU:1, one launch (start us, length us, event | category | flops | bytes accessed | tf_op | source)
XLA Modules:
  0.0 129.6 jit_solution(12544546314154251076)
XLA Ops:
  0.0 0.0 copy-start
  0.0 12.7 %collective-permute-start.2 = (bf16[1536,1536]{1,0:T(8,128)(2,1)}, bf16[1536,1536]{1,0:T(8,128)(2,1)S(1)}, u32[]{:S(2)}, u32[]{:S(2)}) collective-permute-start(bf16[1536,1536]{1,0:T(8,128)(2,1)} %refs_3_.1), channel_id=1, source_target_pairs={{0,4},{4,0},{8,12},{12,8},{16,20},{20,16},{24,28},{28,24},{32,36},... | collective-permute-start | bytes 14155784 | tf_op jit(solution)/shard_map/ppermute | solution.py:187
  12.7 0.0 copy-start.2
  12.7 1.1 copy-done.2
  13.8 0.0 copy-start.3
  13.8 0.7 copy-done.3
  14.4 0.6 shard_map.46
  15.1 12.7 %all_to_all.5.in_ref = bf16[4,48,1536]{2,1,0:T(8,128)(2,1)S(1)} all-to-all(bf16[4,48,1536]{2,1,0:T(8,128)(2,1)S(1)} %shard_map.46), channel_id=1, replica_groups={{0,192,384,576},{64,256,448,640},{128,320,512,704},{1,193,385,577},{65,..., dimensions={0} | all-to-all | bytes 1179648 | tf_op jit(solution)/shard_map/all_to_all | solution.py:189
  27.8 0.8 shard_map.47
  28.6 2.4 %collective-permute-start = (bf16[64,1536]{1,0:T(8,128)(2,1)S(1)}, bf16[64,1536]{1,0:T(8,128)(2,1)S(1)}, u32[]{:S(2)}, u32[]{:S(2)}) collective-permute-start(bf16[64,1536]{1,0:T(8,128)(2,1)S(1)} %get-tuple-element.19), channel_id=1, source_target_pairs={{0,64},{64,128},{128,0},{192,256},{256,320},{320,192},{384,448},{4... | collective-permute-start | bytes 589832 | tf_op jit(solution)/shard_map/ppermute | solution.py:191
  31.0 6.7 %collective-permute-start.1 = (bf16[64,1536]{1,0:T(8,128)(2,1)S(1)}, bf16[64,1536]{1,0:T(8,128)(2,1)S(1)}, u32[]{:S(2)}, u32[]{:S(2)}) collective-permute-start(bf16[64,1536]{1,0:T(8,128)(2,1)S(1)} %get-tuple-element.20), channel_id=1, source_target_pairs={{0,128},{64,0},{128,64},{192,320},{256,192},{320,256},{384,512},{4... | collective-permute-start | bytes 589832 | tf_op jit(solution)/shard_map/ppermute | solution.py:191
  37.8 2.4 %collective-permute-done.refs_1_ = bf16[64,1536]{1,0:T(8,128)(2,1)S(1)} collective-permute-done((bf16[64,1536]{1,0:T(8,128)(2,1)S(1)}, bf16[64,1536]{1,0:T(8,128)(2,1)S(1)}, u32[]{:S(2)}, u32[]{:S(2)}) %collective-permute-start) | collective-permute-done | bytes 196640 | tf_op jit(solution)/shard_map/ppermute | solution.py:191
  40.2 13.9 %collective-permute-done.1.refs_2_ = bf16[64,1536]{1,0:T(8,128)(2,1)S(1)} collective-permute-done((bf16[64,1536]{1,0:T(8,128)(2,1)S(1)}, bf16[64,1536]{1,0:T(8,128)(2,1)S(1)}, u32[]{:S(2)}, u32[]{:S(2)}) %collective-permute-start.1) | collective-permute-done | bytes 196640 | tf_op jit(solution)/shard_map/ppermute | solution.py:191
  54.1 0.7 shard_map.48
  54.8 18.0 %all-gather = bf16[256,1536]{1,0:T(8,128)(2,1)S(1)} all-gather(bf16[64,1536]{1,0:T(8,128)(2,1)S(1)} %shard_map.48), channel_id=2, replica_groups={{0,16,32,48},{4,20,36,52},{8,24,40,56},{12,28,44,60},{1,17,33,49},{5,21..., dimensions={0}, use_global_device_ids=true | all-gather | bytes 983040 | tf_op jit(solution)/shard_map/all_gather | solution.py:193
  72.8 0.1 fusion
  72.9 2.7 %collective-permute-start.6 = (bf16[2,64,1536]{2,1,0:T(8,128)(2,1)S(1)}, bf16[2,64,1536]{2,1,0:T(8,128)(2,1)S(1)}, u32[]{:S(2)}, u32[]{:S(2)}) collective-permute-start(bf16[2,64,1536]{2,1,0:T(8,128)(2,1)S(1)} %bitcast.8), channel_id=1, source_target_pairs={{0,8},{4,12},{8,16},{12,20},{16,24},{20,28},{24,32},{28,36},{32,40... | collective-permute-start | bytes 1179656 | tf_op jit(solution)/shard_map/ppermute | solution.py:195
  75.6 3.8 %collective-permute-start.7 = (bf16[2,64,1536]{2,1,0:T(8,128)(2,1)S(1)}, bf16[2,64,1536]{2,1,0:T(8,128)(2,1)S(1)}, u32[]{:S(2)}, u32[]{:S(2)}) collective-permute-start(bf16[2,64,1536]{2,1,0:T(8,128)(2,1)S(1)} %bitcast.7), channel_id=1, source_target_pairs={{0,56},{4,60},{8,0},{12,4},{16,8},{20,12},{24,16},{28,20},{32,24},... | collective-permute-start | bytes 1179656 | tf_op jit(solution)/shard_map/ppermute | solution.py:196
  79.4 0.0 collective-permute-done.2.refs_1_.refs_2_
  79.4 0.0 copy-done
  79.4 2.6 %shard_map.49 = (bf16[64,3072]{1,0:T(8,128)(2,1)S(1)}, bf16[64,3072]{1,0:T(8,128)(2,1)S(1)}, bf16[64,3072]{1,0:T(8,128)(2,1)S(1)}, bf16[64,3072]{1,0:T(8,128)(2,1)S(1)}) custom-call(bf16[4,64,1536]{2,1,0:T(8,128)(2,1)S(1)} %bitcast.5, bf16[1536,1536]{1,0:T(8,128)(2,1)S(1)} %collective-permute-done.2.refs_1_.refs_2_, bf16[1536,1536]{1,0:T(8,128)(2,1)S(1)} %copy-done), custom_call_target="tpu_custom_call" | custom-call | tf_op jit(solution)/shard_map/pallas_call | solution.py:124
  82.1 8.2 %collective-permute-start.3 = (bf16[64,3072]{1,0:T(8,128)(2,1)S(1)}, bf16[64,3072]{1,0:T(8,128)(2,1)S(1)}, u32[]{:S(2)}, u32[]{:S(2)}) collective-permute-start(bf16[64,3072]{1,0:T(8,128)(2,1)S(1)} %get-tuple-element.23), channel_id=1, source_target_pairs={{0,1},{4,135},{8,9},{12,143},{16,17},{20,151},{24,25},{28,159},{32... | collective-permute-start | bytes 1179656 | tf_op jit(solution)/shard_map/ppermute | solution.py:202
  90.3 1.9 %collective-permute-start.5 = (bf16[64,3072]{1,0:T(8,128)(2,1)S(1)}, bf16[64,3072]{1,0:T(8,128)(2,1)S(1)}, u32[]{:S(2)}, u32[]{:S(2)}) collective-permute-start(bf16[64,3072]{1,0:T(8,128)(2,1)S(1)} %get-tuple-element.24), channel_id=1, source_target_pairs={{0,131},{4,5},{8,139},{12,13},{16,147},{20,21},{24,155},{28,29},{3... | collective-permute-start | bytes 1179656 | tf_op jit(solution)/shard_map/ppermute | solution.py:203
  92.2 0.0 collective-permute-done.6.refs_0_
  92.2 0.0 collective-permute-done.7.refs_1_
  92.2 2.6 %shard_map.50 = (bf16[64,3072]{1,0:T(8,128)(2,1)S(1)}, bf16[64,3072]{1,0:T(8,128)(2,1)S(1)}, bf16[64,3072]{1,0:T(8,128)(2,1)S(1)}, bf16[64,3072]{1,0:T(8,128)(2,1)S(1)}) custom-call(bf16[2,64,1536]{2,1,0:T(8,128)(2,1)S(1)} %collective-permute-done.6.refs_0_, bf16[2,64,1536]{2,1,0:T(8,128)(2,1)S(1)} %collective-permute-done.7.refs_1_, ...), custom_call_target="tpu_custom_call" | custom-call | tf_op jit(solution)/shard_map/pallas_call | solution.py:124
  94.9 0.0 copy-start.1
  94.9 4.7 %collective-permute-start.8 = (bf16[64,3072]{1,0:T(8,128)(2,1)S(1)}, bf16[64,3072]{1,0:T(8,128)(2,1)S(1)}, u32[]{:S(2)}, u32[]{:S(2)}) collective-permute-start(bf16[64,3072]{1,0:T(8,128)(2,1)S(1)} %get-tuple-element.27), channel_id=1, source_target_pairs={{0,1},{4,135},{8,9},{12,143},{16,17},{20,151},{24,25},{28,159},{32... | collective-permute-start | bytes 1179656 | tf_op jit(solution)/shard_map/ppermute | solution.py:202
  99.6 1.9 %collective-permute-start.10 = (bf16[64,3072]{1,0:T(8,128)(2,1)S(1)}, bf16[64,3072]{1,0:T(8,128)(2,1)S(1)}, u32[]{:S(2)}, u32[]{:S(2)}) collective-permute-start(bf16[64,3072]{1,0:T(8,128)(2,1)S(1)} %get-tuple-element.28), channel_id=1, source_target_pairs={{0,131},{4,5},{8,139},{12,13},{16,147},{20,21},{24,155},{28,29},{3... | collective-permute-start | bytes 1179656 | tf_op jit(solution)/shard_map/ppermute | solution.py:203
  101.5 0.0 collective-permute-done.3
  101.5 0.1 add_convert_fusion.1
  101.6 4.6 %collective-permute-start.4 = (bf16[64,3072]{1,0:T(8,128)(2,1)S(1)}, bf16[64,3072]{1,0:T(8,128)(2,1)S(1)}, u32[]{:S(2)}, u32[]{:S(2)}) collective-permute-start(bf16[64,3072]{1,0:T(8,128)(2,1)S(1)} %add_convert_fusion.1), channel_id=1, source_target_pairs={{0,1},{4,135},{8,9},{12,143},{16,17},{20,151},{24,25},{28,159},{32... | collective-permute-start | bytes 1179656 | tf_op jit(solution)/shard_map/ppermute | solution.py:205
  106.2 0.6 collective-permute-done.8
  106.8 0.1 add_convert_fusion
  106.9 5.0 %collective-permute-start.9 = (bf16[64,3072]{1,0:T(8,128)(2,1)S(1)}, bf16[64,3072]{1,0:T(8,128)(2,1)S(1)}, u32[]{:S(2)}, u32[]{:S(2)}) collective-permute-start(bf16[64,3072]{1,0:T(8,128)(2,1)S(1)} %add_convert_fusion), channel_id=1, source_target_pairs={{0,1},{4,135},{8,9},{12,143},{16,17},{20,151},{24,25},{28,159},{32... | collective-permute-start | bytes 1179656 | tf_op jit(solution)/shard_map/ppermute | solution.py:205
  111.9 0.0 collective-permute-done.5.refs_2_
  111.9 0.5 collective-permute-done.10.refs_5_
  112.4 1.3 collective-permute-done.4.refs_1_
  113.7 5.7 %collective-permute-done.9.refs_4_ = bf16[64,3072]{1,0:T(8,128)(2,1)S(1)} collective-permute-done((bf16[64,3072]{1,0:T(8,128)(2,1)S(1)}, bf16[64,3072]{1,0:T(8,128)(2,1)S(1)}, u32[]{:S(2)}, u32[]{:S(2)}) %collective-permute-start.9) | collective-permute-done | bytes 393248 | tf_op jit(solution)/shard_map/ppermute | solution.py:205
  119.4 0.1 shard_map.52
  119.5 7.7 %collective-permute-start.11 = (bf16[2,4,16,1536]{3,2,1,0:T(8,128)(2,1)S(1)}, bf16[2,4,16,1536]{3,2,1,0:T(8,128)(2,1)S(1)}, u32[]{:S(2)}, u32[]{:S(2)}) collective-permute-start(bf16[2,4,16,1536]{3,2,1,0:T(8,128)(2,1)S(1)} %shard_map.52), channel_id=1, source_target_pairs={{0,4},{4,0},{8,12},{12,8},{16,20},{20,16},{24,28},{28,24},{32,36},... | collective-permute-start | bytes 1179656 | tf_op jit(solution)/shard_map/ppermute | solution.py:219
  127.3 0.0 copy-done.1
  127.3 0.8 shard_map.51
  128.1 0.5 collective-permute-done.11.other_ref
  128.6 1.0 shard_map.53
Async XLA Ops:
  0.0 79.4 %copy-start = (bf16[1536,1536]{1,0:T(8,128)(2,1)S(1)}, bf16[1536,1536]{1,0:T(8,128)(2,1)}, u32[]{:S(2)}) copy-start(bf16[1536,1536]{1,0:T(8,128)(2,1)} %refs_3_.1) | copy-start | bytes 14155780
  0.0 79.4 %collective-permute-start.2 = (bf16[1536,1536]{1,0:T(8,128)(2,1)}, bf16[1536,1536]{1,0:T(8,128)(2,1)S(1)}, u32[]{:S(2)}, u32[]{:S(2)}) collective-permute-start(bf16[1536,1536]{1,0:T(8,128)(2,1)} %refs_3_.1), channel_id=1, source_target_pairs={{0,4},{4,0},{8,12},{12,8},{16,20},{20,16},{24,28},{28,24},{32,36},... | collective-permute-start | bytes 14155784 | tf_op jit(solution)/shard_map/ppermute | solution.py:187
  12.7 1.1 copy-start.2
  13.8 0.7 copy-start.3
  28.6 11.6 %collective-permute-start = (bf16[64,1536]{1,0:T(8,128)(2,1)S(1)}, bf16[64,1536]{1,0:T(8,128)(2,1)S(1)}, u32[]{:S(2)}, u32[]{:S(2)}) collective-permute-start(bf16[64,1536]{1,0:T(8,128)(2,1)S(1)} %get-tuple-element.19), channel_id=1, source_target_pairs={{0,64},{64,128},{128,0},{192,256},{256,320},{320,192},{384,448},{4... | collective-permute-start | bytes 589832 | tf_op jit(solution)/shard_map/ppermute | solution.py:191
  31.0 23.1 %collective-permute-start.1 = (bf16[64,1536]{1,0:T(8,128)(2,1)S(1)}, bf16[64,1536]{1,0:T(8,128)(2,1)S(1)}, u32[]{:S(2)}, u32[]{:S(2)}) collective-permute-start(bf16[64,1536]{1,0:T(8,128)(2,1)S(1)} %get-tuple-element.20), channel_id=1, source_target_pairs={{0,128},{64,0},{128,64},{192,320},{256,192},{320,256},{384,512},{4... | collective-permute-start | bytes 589832 | tf_op jit(solution)/shard_map/ppermute | solution.py:191
  72.9 19.3 %collective-permute-start.6 = (bf16[2,64,1536]{2,1,0:T(8,128)(2,1)S(1)}, bf16[2,64,1536]{2,1,0:T(8,128)(2,1)S(1)}, u32[]{:S(2)}, u32[]{:S(2)}) collective-permute-start(bf16[2,64,1536]{2,1,0:T(8,128)(2,1)S(1)} %bitcast.8), channel_id=1, source_target_pairs={{0,8},{4,12},{8,16},{12,20},{16,24},{20,28},{24,32},{28,36},{32,40... | collective-permute-start | bytes 1179656 | tf_op jit(solution)/shard_map/ppermute | solution.py:195
  75.6 16.6 %collective-permute-start.7 = (bf16[2,64,1536]{2,1,0:T(8,128)(2,1)S(1)}, bf16[2,64,1536]{2,1,0:T(8,128)(2,1)S(1)}, u32[]{:S(2)}, u32[]{:S(2)}) collective-permute-start(bf16[2,64,1536]{2,1,0:T(8,128)(2,1)S(1)} %bitcast.7), channel_id=1, source_target_pairs={{0,56},{4,60},{8,0},{12,4},{16,8},{20,12},{24,16},{28,20},{32,24},... | collective-permute-start | bytes 1179656 | tf_op jit(solution)/shard_map/ppermute | solution.py:196
  82.1 19.4 %collective-permute-start.3 = (bf16[64,3072]{1,0:T(8,128)(2,1)S(1)}, bf16[64,3072]{1,0:T(8,128)(2,1)S(1)}, u32[]{:S(2)}, u32[]{:S(2)}) collective-permute-start(bf16[64,3072]{1,0:T(8,128)(2,1)S(1)} %get-tuple-element.23), channel_id=1, source_target_pairs={{0,1},{4,135},{8,9},{12,143},{16,17},{20,151},{24,25},{28,159},{32... | collective-permute-start | bytes 1179656 | tf_op jit(solution)/shard_map/ppermute | solution.py:202
  90.3 21.6 %collective-permute-start.5 = (bf16[64,3072]{1,0:T(8,128)(2,1)S(1)}, bf16[64,3072]{1,0:T(8,128)(2,1)S(1)}, u32[]{:S(2)}, u32[]{:S(2)}) collective-permute-start(bf16[64,3072]{1,0:T(8,128)(2,1)S(1)} %get-tuple-element.24), channel_id=1, source_target_pairs={{0,131},{4,5},{8,139},{12,13},{16,147},{20,21},{24,155},{28,29},{3... | collective-permute-start | bytes 1179656 | tf_op jit(solution)/shard_map/ppermute | solution.py:203
  94.9 32.4 %copy-start.1 = (bf16[256,1536]{1,0:T(8,128)(2,1)S(1)}, bf16[256,1536]{1,0:T(8,128)(2,1)}, u32[]{:S(2)}) copy-start(bf16[256,1536]{1,0:T(8,128)(2,1)} %param.7) | copy-start | bytes 2359300
  94.9 11.9 %collective-permute-start.8 = (bf16[64,3072]{1,0:T(8,128)(2,1)S(1)}, bf16[64,3072]{1,0:T(8,128)(2,1)S(1)}, u32[]{:S(2)}, u32[]{:S(2)}) collective-permute-start(bf16[64,3072]{1,0:T(8,128)(2,1)S(1)} %get-tuple-element.27), channel_id=1, source_target_pairs={{0,1},{4,135},{8,9},{12,143},{16,17},{20,151},{24,25},{28,159},{32... | collective-permute-start | bytes 1179656 | tf_op jit(solution)/shard_map/ppermute | solution.py:202
  99.6 12.8 %collective-permute-start.10 = (bf16[64,3072]{1,0:T(8,128)(2,1)S(1)}, bf16[64,3072]{1,0:T(8,128)(2,1)S(1)}, u32[]{:S(2)}, u32[]{:S(2)}) collective-permute-start(bf16[64,3072]{1,0:T(8,128)(2,1)S(1)} %get-tuple-element.28), channel_id=1, source_target_pairs={{0,131},{4,5},{8,139},{12,13},{16,147},{20,21},{24,155},{28,29},{3... | collective-permute-start | bytes 1179656 | tf_op jit(solution)/shard_map/ppermute | solution.py:203
  101.6 12.1 %collective-permute-start.4 = (bf16[64,3072]{1,0:T(8,128)(2,1)S(1)}, bf16[64,3072]{1,0:T(8,128)(2,1)S(1)}, u32[]{:S(2)}, u32[]{:S(2)}) collective-permute-start(bf16[64,3072]{1,0:T(8,128)(2,1)S(1)} %add_convert_fusion.1), channel_id=1, source_target_pairs={{0,1},{4,135},{8,9},{12,143},{16,17},{20,151},{24,25},{28,159},{32... | collective-permute-start | bytes 1179656 | tf_op jit(solution)/shard_map/ppermute | solution.py:205
  106.9 12.5 %collective-permute-start.9 = (bf16[64,3072]{1,0:T(8,128)(2,1)S(1)}, bf16[64,3072]{1,0:T(8,128)(2,1)S(1)}, u32[]{:S(2)}, u32[]{:S(2)}) collective-permute-start(bf16[64,3072]{1,0:T(8,128)(2,1)S(1)} %add_convert_fusion), channel_id=1, source_target_pairs={{0,1},{4,135},{8,9},{12,143},{16,17},{20,151},{24,25},{28,159},{32... | collective-permute-start | bytes 1179656 | tf_op jit(solution)/shard_map/ppermute | solution.py:205
  119.5 9.0 %collective-permute-start.11 = (bf16[2,4,16,1536]{3,2,1,0:T(8,128)(2,1)S(1)}, bf16[2,4,16,1536]{3,2,1,0:T(8,128)(2,1)S(1)}, u32[]{:S(2)}, u32[]{:S(2)}) collective-permute-start(bf16[2,4,16,1536]{3,2,1,0:T(8,128)(2,1)S(1)} %shard_map.52), channel_id=1, source_target_pairs={{0,4},{4,0},{8,12},{12,8},{16,20},{20,16},{24,28},{28,24},{32,36},... | collective-permute-start | bytes 1179656 | tf_op jit(solution)/shard_map/ppermute | solution.py:219
